TPU v7x, 512 devices: a whole 4x4x16 slice. The times are simulated.
512 devices in a mesh: row: 64 (over x, z), col: 8 (over y, core).
Axes of the slice: x: 4, y: 4, z: 16, core: 2. Of those that a mesh axis runs over, the one named last changes fastest.
Arguments:
- omega_tiles: float32 [512, 24, 128, 128], P('row', 'col'), may hold values from -0.3 to 0.3
- omega_diag: float32 [65536, 128], P(('row', 'col')), may hold values from -0.25 to 2, as said below
- samples: float32 [65536, 128], P(('row', 'col')), may hold values from -6 to 6
- pattern: int32 [512, 24], P('row', 'col'), may hold values from 0 to 511, as said below
Outputs:
- next_tiles: float32 [512, 24, 128, 128], P('row', 'col')
- next_diag: float32 [65536, 128], P(('row', 'col'))
Inputs may be any that keep to these rules, and one draw needn't show every extreme that they name: `pattern`: block j stands at slot s of block row i exactly when block i stands at slot s of block row j, and never in the same group of 8 block rows as i. For the block rows of one index of row and the 3 slots of one index of col, at most 1 listed blocks fall in the block rows of any one other index of row, and exactly 1 for some. A block may stand at more than one slot of a row. `omega_diag`: each row's entry on the diagonal of its block lies in 1 to 2; the others lie within -0.25 to 0.25.
All inputs are finite; a program needn't handle non-finite values.
Results may differ from a plain program's by a relative error of at most 0.00012.
Values sent between devices are 32-bit elements; how exact they have to be, the bound alone decides.
No kernel may reach another device: no remote copies, remote signals or barrier semaphores. Data moves between devices by JAX's collectives and lax.ppermute only.
A program may use at most 64 MiB of HBM per device.

v0:
```python
import jax
import jax.numpy as jnp
from jax import lax
from jax.sharding import PartitionSpec as P

ITERS = 2


step_size = 0.2
shrink_weight = 0.05
ridge_weight = 0.1


def sent_to_all(value, axis):
    copies = jnp.broadcast_to(value, (lax.axis_size(axis), *value.shape))
    return lax.all_to_all(copies, axis, split_axis=0, concat_axis=0, tiled=True)


def joined_along(tiles, dim):
    dims = list(tiles.shape[1:])
    dims[dim] *= tiles.shape[0]
    return jnp.moveaxis(tiles, 0, dim).reshape(dims)


def gathered_copies(value, axis, dim):
    tiles = sent_to_all(value, axis)
    return joined_along(tiles, dim)


def over_pieces(value, axis):
    tiles = lax.all_gather(value, axis)
    return tiles.sum(axis=0)


def soft_shrink(values, threshold):
    return values - jnp.clip(values, -threshold, threshold)


def on_device(omega_tiles, omega_diag, samples, pattern):
    highest = lax.Precision.HIGHEST
    row_count = lax.axis_size("row")
    col_count = lax.axis_size("col")
    my_row = lax.axis_index("row")
    my_col = lax.axis_index("col")
    block_rows = omega_tiles.shape[0]
    slot_count = omega_tiles.shape[1]
    block_size = omega_tiles.shape[2]
    sample_count = samples.shape[1]
    diag_blocks = block_rows // col_count
    all_blocks = block_rows * row_count
    peer_span = row_count // 2 - 2
    capacity = max(1, (slot_count * block_rows // 2 - 1 + peer_span - 1) // peer_span)
    tile_count = block_rows * slot_count
    x_rows = gathered_copies(samples, "col", 0)
    x_blocks = x_rows.reshape(block_rows, block_size, sample_count)
    slot_ids = my_col * slot_count + jnp.arange(slot_count, dtype=jnp.int32)
    own_blocks = my_row * block_rows + jnp.arange(block_rows, dtype=jnp.int32)
    peer_row = (pattern // block_rows).reshape(tile_count)
    order_key = (
        slot_ids[None, :] * all_blocks + jnp.minimum(own_blocks[:, None], pattern)
    ).reshape(tile_count)
    same_peer = peer_row[:, None] == peer_row[None, :]
    before = order_key[None, :] < order_key[:, None]
    peer_rank = jnp.sum((same_peer & before).astype(jnp.int32), axis=1)
    dest_slot = peer_row * capacity + peer_rank
    source_row = jnp.arange(tile_count, dtype=jnp.int32) // slot_count

    def pack_slots(values):
        empty_slots = jnp.zeros((row_count * capacity,) + values.shape[1:], jnp.float32)
        return empty_slots.at[dest_slot].set(values)

    def unpack_slots(received):
        return received[dest_slot].reshape((block_rows, slot_count) + received.shape[1:])

    x_tiles = unpack_slots(
        lax.all_to_all(
            pack_slots(x_blocks[source_row]), "row", split_axis=0, concat_axis=0, tiled=True
        )
    )
    first_diag = my_col * diag_blocks
    x_diag = lax.dynamic_slice_in_dim(x_blocks, first_diag, diag_blocks, 0)
    identity = jnp.eye(block_size, dtype=jnp.float32)
    tile_vals = omega_tiles
    diag_vals = omega_diag.reshape(diag_blocks, block_size, block_size)
    for sweep_index in range(ITERS):
        row_terms = jnp.einsum("askm,asmn->akn", tile_vals, x_tiles, precision=highest)
        diag_terms = jnp.einsum("bkm,bmn->bkn", diag_vals, x_diag, precision=highest)
        own_terms = lax.dynamic_slice_in_dim(row_terms, first_diag, diag_blocks, 0) + diag_terms
        row_terms = lax.dynamic_update_slice_in_dim(row_terms, own_terms, first_diag, 0)
        products = over_pieces(row_terms, "col")
        cross_terms = jnp.einsum("akn,asqn->askq", products, x_tiles, precision=highest)
        returned = lax.all_to_all(
            pack_slots(products[source_row]), "row", split_axis=0, concat_axis=0, tiled=True
        )
        mirror = jnp.einsum("akn,asqn->askq", x_blocks, unpack_slots(returned), precision=highest)
        gradient = (cross_terms + mirror) * (0.5 / sample_count) + ridge_weight * tile_vals
        tile_vals = soft_shrink(tile_vals - step_size * gradient, step_size * shrink_weight)
        y_diag = lax.dynamic_slice_in_dim(products, first_diag, diag_blocks, 0)
        self_cross = jnp.einsum("bkn,bqn->bkq", y_diag, x_diag, precision=highest)
        pivots = jnp.diagonal(diag_vals, axis1=1, axis2=2)
        diag_grad = (self_cross + jnp.swapaxes(self_cross, 1, 2)) * (
            0.5 / sample_count
        ) + ridge_weight * diag_vals
        diag_grad = diag_grad - identity * (1.0 / pivots)[:, :, None]
        stepped = diag_vals - step_size * diag_grad
        diag_vals = identity * stepped + (1.0 - identity) * soft_shrink(
            stepped, step_size * shrink_weight
        )
    return (tile_vals, diag_vals.reshape(omega_diag.shape))


def solution(mesh):
    in_specs = (
        P("row", "col", None, None),
        P(("row", "col"), None),
        P(("row", "col"), None),
        P("row", "col"),
    )
    out_specs = (P("row", "col", None, None), P(("row", "col"), None))
    return jax.shard_map(
        on_device, mesh=mesh, in_specs=in_specs, out_specs=out_specs, check_vma=False
    )
```

profile of v0, /device:TPU:1, one launch (start us, length us, event | category | flops | bytes accessed | tf_op | source)
XLA Modules:
  0.0 775.8 jit_solution(13486683686394685017)
XLA Ops:
  7.2 1.7 broadcast_in_dim.6
  8.8 10.3 %all-to-all-start = ((f32[8,128,128]{2,1,0:T(8,128)}), f32[8,128,128]{2,1,0:T(8,128)S(1)}, u32[]{:S(2)}, u32[]{:S(2)}) async-start(f32[8,128,128]{2,1,0:T(8,128)} %broadcast_in_dim.6), calls=%async_computation | async-start | bytes 1048576 | tf_op jit(solution)/shard_map/all_to_all | solution.py:16
  19.6 0.2 convert_reduce_fusion
  19.8 8.8 %all-to-all-done = f32[8,128,128]{2,1,0:T(8,128)S(1)} async-done(((f32[8,128,128]{2,1,0:T(8,128)}), f32[8,128,128]{2,1,0:T(8,128)S(1)}, u32[]{:S(2)}, u32[]{:S(2)}) %all-to-all-start) | async-done | bytes 524320 | tf_op jit(solution)/shard_map/all_to_all | solution.py:16
  28.6 0.6 gather_fusion
  29.3 2.5 broadcast.218.clone
  31.8 5.6 scatter_fusion
  37.4 14.3 %all-to-all-start.1 = ((f32[64,128,128]{2,1,0:T(8,128)}), f32[64,128,128]{2,1,0:T(8,128)}, u32[]{:S(2)}, u32[]{:S(2)}) async-start(f32[64,128,128]{2,1,0:T(8,128)} %scatter_fusion), calls=%async_computation.1 | async-start | bytes 8388608 | tf_op jit(solution)/shard_map/all_to_all | solution.py:76
  51.7 182.1 %all-to-all-done.1 = f32[64,128,128]{2,1,0:T(8,128)} async-done(((f32[64,128,128]{2,1,0:T(8,128)}), f32[64,128,128]{2,1,0:T(8,128)}, u32[]{:S(2)}, u32[]{:S(2)}) %all-to-all-start.1) | async-done | bytes 4194336 | tf_op jit(solution)/shard_map/all_to_all | solution.py:76
  233.8 2.8 gather_fusion.1
  236.7 4.2 fusion.52
  240.9 0.3 fusion.6
  241.2 1.0 copy.61
  242.3 37.7 %all-gather.3.cloned.1.call-done = f32[8,8,128,128]{3,2,1,0:T(8,128)} async-done(((f32[1,8,128,128]{3,2,1,0:T(8,128)}), f32[8,8,128,128]{3,2,1,0:T(8,128)}) %all-gather.3.cloned.1.call-update) | async-done | bytes 4194320 | tf_op jit(solution)/shard_map/all_gather | solution.py:31
  280.0 2.5 reduce_sum.31
  282.5 0.2 copy.82
  282.7 1.8 gather_fusion.2
  284.5 3.0 copy.64
  287.5 2.5 broadcast.218.clone.1
  290.0 6.1 scatter_fusion.1
  296.1 15.7 %all-to-all-start.2 = ((f32[64,128,128]{2,1,0:T(8,128)}), f32[64,128,128]{2,1,0:T(8,128)}, u32[]{:S(2)}, u32[]{:S(2)}) async-start(f32[64,128,128]{2,1,0:T(8,128)} %scatter_fusion.1), calls=%async_computation.2 | async-start | bytes 8388608 | tf_op jit(solution)/shard_map/all_to_all | solution.py:92
  311.8 0.2 all-gather.5.cloned.1.call-start
  312.0 3.0 copy.66
  315.0 1.2 gather_fusion.4
  316.3 0.3 convolution_bitcast_fusion.1
  316.7 0.1 fusion.17
  316.8 2.7 fusion.10
  319.5 176.4 %all-to-all-done.2 = f32[64,128,128]{2,1,0:T(8,128)} async-done(((f32[64,128,128]{2,1,0:T(8,128)}), f32[64,128,128]{2,1,0:T(8,128)}, u32[]{:S(2)}, u32[]{:S(2)}) %all-to-all-start.2) | async-done | bytes 4194336 | tf_op jit(solution)/shard_map/all_to_all | solution.py:92
  495.9 4.0 gather_fusion.3
  499.9 4.2 clamp_subtract_fusion.1
  504.1 2.8 fusion.53
  507.0 0.2 fusion.9
  507.2 0.8 copy-done.3
  508.0 36.3 %all-gather.5.cloned.1.call-done = f32[8,8,128,128]{3,2,1,0:T(8,128)} async-done(((f32[1,8,128,128]{3,2,1,0:T(8,128)}), f32[8,8,128,128]{3,2,1,0:T(8,128)}) %all-gather.5.cloned.1.call-update) | async-done | bytes 4194320 | tf_op jit(solution)/shard_map/all_gather | solution.py:31
  544.3 2.5 reduce_sum.32
  546.8 1.8 gather_fusion.5
  548.6 2.5 broadcast.218
  551.1 6.1 scatter_fusion.2
  557.3 15.9 %all-to-all-start.3 = ((f32[64,128,128]{2,1,0:T(8,128)}), f32[64,128,128]{2,1,0:T(8,128)}, u32[]{:S(2)}, u32[]{:S(2)}) async-start(f32[64,128,128]{2,1,0:T(8,128)} %scatter_fusion.2), calls=%async_computation.3 | async-start | bytes 8388608 | tf_op jit(solution)/shard_map/all_to_all | solution.py:92
  573.2 1.2 gather_fusion.7
  574.4 0.3 fusion.26
  574.7 0.1 copy.70
  574.8 0.7 fusion.20
  575.5 2.7 fusion.12
  578.2 178.8 %all-to-all-done.3 = f32[64,128,128]{2,1,0:T(8,128)} async-done(((f32[64,128,128]{2,1,0:T(8,128)}), f32[64,128,128]{2,1,0:T(8,128)}, u32[]{:S(2)}, u32[]{:S(2)}) %all-to-all-start.3) | async-done | bytes 4194336 | tf_op jit(solution)/shard_map/all_to_all | solution.py:92
  757.0 4.0 gather_fusion.6
  761.1 4.9 clamp_subtract_fusion
  766.0 3.0 copy.71
  (29 shorter events, 0.8 us)
Async XLA Ops:
  7.2 12.0 %copy-start.4 = (s32[8,3]{0,1:T(4,128)S(1)}, s32[8,3]{0,1:T(4,128)}, u32[]{:S(2)}) copy-start(s32[8,3]{0,1:T(4,128)} %param.7) | copy-start | bytes 292
  8.8 19.8 %all-to-all-start = ((f32[8,128,128]{2,1,0:T(8,128)}), f32[8,128,128]{2,1,0:T(8,128)S(1)}, u32[]{:S(2)}, u32[]{:S(2)}) async-start(f32[8,128,128]{2,1,0:T(8,128)} %broadcast_in_dim.6), calls=%async_computation | async-start | bytes 1048576 | tf_op jit(solution)/shard_map/all_to_all | solution.py:16
  37.4 196.4 %all-to-all-start.1 = ((f32[64,128,128]{2,1,0:T(8,128)}), f32[64,128,128]{2,1,0:T(8,128)}, u32[]{:S(2)}, u32[]{:S(2)}) async-start(f32[64,128,128]{2,1,0:T(8,128)} %scatter_fusion), calls=%async_computation.1 | async-start | bytes 8388608 | tf_op jit(solution)/shard_map/all_to_all | solution.py:76
  51.7 228.3 %all-gather.3.cloned.1.call-start = ((), (), s32[]{:S(2)}) async-start(), calls=%async_computation.4 | async-start | bytes 4718592 | tf_op jit(solution)/shard_map/all_gather | solution.py:31
  236.7 4.3 copy-start.2
  296.1 199.8 %all-to-all-start.2 = ((f32[64,128,128]{2,1,0:T(8,128)}), f32[64,128,128]{2,1,0:T(8,128)}, u32[]{:S(2)}, u32[]{:S(2)}) async-start(f32[64,128,128]{2,1,0:T(8,128)} %scatter_fusion.1), calls=%async_computation.2 | async-start | bytes 8388608 | tf_op jit(solution)/shard_map/all_to_all | solution.py:92
  311.8 232.5 %all-gather.5.cloned.1.call-start = ((), (), s32[]{:S(2)}) async-start(), calls=%async_computation.5 | async-start | bytes 4718592 | tf_op jit(solution)/shard_map/all_gather | solution.py:31
  504.1 2.8 copy-start
  507.2 0.8 copy-start.3
  557.3 199.8 %all-to-all-start.3 = ((f32[64,128,128]{2,1,0:T(8,128)}), f32[64,128,128]{2,1,0:T(8,128)}, u32[]{:S(2)}, u32[]{:S(2)}) async-start(f32[64,128,128]{2,1,0:T(8,128)} %scatter_fusion.2), calls=%async_computation.3 | async-start | bytes 8388608 | tf_op jit(solution)/shard_map/all_to_all | solution.py:92
  578.2 182.8 %copy-start.1 = (f32[8,3,128,128]{2,3,1,0:T(8,128)S(1)}, f32[8,3,128,128]{2,3,1,0:T(8,128)}, u32[]{:S(2)}) copy-start(f32[8,3,128,128]{2,3,1,0:T(8,128)} %copy-done) | copy-start | bytes 4718596
Sparse Core Ops, SparseCore 0:
  242.4 37.5 all-gather.2
  508.2 36.1 all-gather.4
where the time goes:
time: 779 us; the launch traced here: 776 us
  waiting for transfers between devices  620 us (80%)
  starting transfers between devices  56.4 us (7%)
  local copies, waits for them, and re-layouts  56.3 us (7%)
  matrix products  22.7 us (3%)
  between operations  14.3 us (2%)
    all_to_all x2, waiting for transfers between devices, on_device(): lax.all_to_all(pack_slots(products[source_row]), 'row', split_axis=0, con...  355 us
    all_to_all x1, waiting for transfers between devices, on_device(): lax.all_to_all(pack_slots(x_blocks[source_row]), 'row', split_axis=0, con...  182 us
    all_gather x2, waiting for transfers between devices, over_pieces(): tiles = lax.all_gather(value, axis)  74 us
    all_to_all x2, starting transfers between devices, on_device(): lax.all_to_all(pack_slots(products[source_row]), 'row', split_axis=0, con...  31.5 us
    scatter x3, local copies, waits for them, and re-layouts, pack_slots(): return empty_slots.at[dest_slot].set(values)  17.9 us
  transfers between devices with their start and end apart: 6, of which 6 were waited for; matrix products, arithmetic and copies ran while one was open for 2% of the time, Pallas kernels for 0%

commit v1 on v0

v1 whole, which is shorter than its diff:
```python
import jax
import jax.numpy as jnp
from jax import lax
from jax.experimental import pallas as pl
from jax.experimental.pallas import tpu as pltpu
from jax.sharding import Mesh
from jax.sharding import PartitionSpec as P

ITERS = 2
STEP = 0.2
SHRINK = 0.05
RIDGE = 0.1

BS = 128
ROWS = 8
SLOTS = 3
TILES = ROWS * SLOTS
WANT = TILES + ROWS

X, Z, Y, CORE = 4, 16, 4, 2
ZL = 2
ZH = Z // ZL
COL = ("y", "k")
PEERS = ("x", "zl", "y", "k")
NP = X * ZL * Y * CORE
Q = BS // NP
GROUPS = NP // ROWS
TABLE = ZH * NP

VMEM = 48 * 1024 * 1024


def split(v):
    hi = v.astype(jnp.bfloat16)
    lo = (v - hi.astype(jnp.float32)).astype(jnp.bfloat16)
    return hi, lo


def dot(a, b, rhs_dim):
    return lax.dot_general(
        a, b, (((1,), (rhs_dim,)), ((), ())), preferred_element_type=jnp.float32
    )


def dot3(a, b, rhs_dim):
    return dot(a[0], b[0], rhs_dim) + (dot(a[0], b[1], rhs_dim) + dot(a[1], b[0], rhs_dim))


def shrink(v):
    t = STEP * SHRINK
    return v - jnp.clip(v, -t, t)


def select_kernel(idx, table, out, *, dests):
    first = pl.program_id(0) * dests

    def one(d, carry):
        base = (first + d) * WANT
        for t in range(WANT):
            out[d, t] = table[idx[base + t]]
        return carry

    lax.fori_loop(0, dests, one, 0)


def select(idx, table):
    dests = 8
    return pl.pallas_call(
        lambda i, t, o: select_kernel(i, t, o, dests=dests),
        grid_spec=pltpu.PrefetchScalarGridSpec(
            num_scalar_prefetch=1,
            grid=(NP // dests,),
            in_specs=[pl.BlockSpec((TABLE, Q, BS), lambda g, i: (0, 0, 0))],
            out_specs=pl.BlockSpec((dests, WANT, Q, BS), lambda g, i: (g, 0, 0, 0)),
        ),
        out_shape=jax.ShapeDtypeStruct((NP, WANT, Q, BS), jnp.float32),
        compiler_params=pltpu.CompilerParams(vmem_limit_bytes=VMEM),
    )(idx, table)


def assembled(recv, t):
    parts = [recv[pl.ds(t * Q + q, NP, stride=WANT * Q), :] for q in range(Q)]
    return jnp.concatenate(parts, axis=0)


def spread(out, i, value):
    for q in range(Q):
        out[pl.ds(i * Q + q, NP, stride=ROWS * Q), :] = value[q * NP : (q + 1) * NP]


def stacked(pairs, axis):
    return tuple(jnp.concatenate([p[n] for p in pairs], axis=axis) for n in range(2))


def first_kernel(col, recv, tiles, diag, xj, xi, sums):
    i = pl.program_id(0)
    xs = []
    for s in range(SLOTS):
        x = split(assembled(recv, i * SLOTS + s))
        xs.append(x)
        xj[0, s], xj[1, s] = x
    own = split(assembled(recv, TILES + i))
    xi[0, 0], xi[1, 0] = own
    bs = [split(tiles[0, s]) for s in range(SLOTS)]
    total = dot3(stacked(bs, 1), stacked(xs, 0), 0)
    spread(sums, i, total)

    @pl.when(i == col[0])
    def _():
        spread(sums, i, total + dot3(split(diag[...]), own, 0))


def sweep_kernel(col, recv, tiles, diag, xj, xi, new_tiles, new_diag, *rest):
    i = pl.program_id(0)
    own_x = (xi[0, 0], xi[1, 0])
    own_y = split(assembled(recv, TILES + i))
    lhs = stacked([own_y, own_x], 1)
    bs, xs = [], []
    for s in range(SLOTS):
        x = (xj[0, s], xj[1, s])
        y = split(assembled(recv, i * SLOTS + s))
        cross = dot3(lhs, stacked([x, y], 1), 1)
        old = tiles[0, s]
        new = shrink(old - STEP * (cross * (0.5 / BS) + RIDGE * old))
        new_tiles[0, s] = new
        if rest:
            bs.append(split(new))
            xs.append(x)
    if rest:
        total = dot3(stacked(bs, 1), stacked(xs, 0), 0)
        spread(rest[0], i, total)

    @pl.when(i == col[0])
    def _():
        cross = dot3(lhs, stacked([own_x, own_y], 1), 1)
        old = diag[...]
        shape = (BS, BS)
        eye = lax.broadcasted_iota(jnp.int32, shape, 0) == lax.broadcasted_iota(
            jnp.int32, shape, 1
        )
        pivots = jnp.where(eye, 1.0 / jnp.where(eye, old, 1.0), 0.0)
        stepped = old - STEP * (cross * (0.5 / BS) + RIDGE * old - pivots)
        new = jnp.where(eye, stepped, shrink(stepped))
        new_diag[...] = new
        if rest:
            spread(rest[0], i, total + dot3(split(new), own_x, 0))


whole_recv = pl.BlockSpec((NP * WANT * Q, BS), lambda i, c: (0, 0))
tile_spec = pl.BlockSpec((1, SLOTS, BS, BS), lambda i, c: (i, 0, 0, 0))
diag_spec = pl.BlockSpec((BS, BS), lambda i, c: (0, 0))
xj_spec = pl.BlockSpec((2, SLOTS, BS, BS), lambda i, c: (0, i, 0, 0))
xi_spec = pl.BlockSpec((2, 1, BS, BS), lambda i, c: (0, i, 0, 0))
sums_spec = pl.BlockSpec((NP * ROWS * Q, BS), lambda i, c: (0, 0))
xj_shape = jax.ShapeDtypeStruct((2, TILES, BS, BS), jnp.bfloat16)
xi_shape = jax.ShapeDtypeStruct((2, ROWS, BS, BS), jnp.bfloat16)
sums_shape = jax.ShapeDtypeStruct((NP * ROWS * Q, BS), jnp.float32)
tiles_shape = jax.ShapeDtypeStruct((ROWS, SLOTS, BS, BS), jnp.float32)
diag_shape = jax.ShapeDtypeStruct((BS, BS), jnp.float32)


def call(kernel, in_specs, out_specs, out_shape):
    return pl.pallas_call(
        kernel,
        grid_spec=pltpu.PrefetchScalarGridSpec(
            num_scalar_prefetch=1, grid=(ROWS,), in_specs=in_specs, out_specs=out_specs
        ),
        out_shape=out_shape,
        compiler_params=pltpu.CompilerParams(vmem_limit_bytes=VMEM),
    )


first_call = call(
    first_kernel,
    [whole_recv, tile_spec, diag_spec],
    [xj_spec, xi_spec, sums_spec],
    [xj_shape, xi_shape, sums_shape],
)
sweep_ins = [whole_recv, tile_spec, diag_spec, xj_spec, xi_spec]
sweep_call = call(
    sweep_kernel,
    sweep_ins,
    [tile_spec, diag_spec, sums_spec],
    [tiles_shape, diag_shape, sums_shape],
)
last_call = call(sweep_kernel, sweep_ins, [tile_spec, diag_spec], [tiles_shape, diag_shape])


def swapped(value):
    return lax.all_to_all(value, PEERS, split_axis=0, concat_axis=0, tiled=True)


def on_device(omega_tiles, omega_diag, samples, pattern):
    col = lax.axis_index(COL).astype(jnp.int32).reshape(1)
    row, member = pattern // ROWS, pattern % ROWS
    place = (row % Z) // ZL * NP + (row // Z * ZL + row % ZL) * ROWS + member
    place = place.astype(jnp.float32).reshape(1, 1, TILES)
    place = jnp.broadcast_to(
        jnp.pad(place, ((0, 0), (0, 0), (0, BS - TILES))), (NP, 1, BS)
    )
    pieces = jnp.swapaxes(samples.reshape(Q, NP, BS), 0, 1)
    came = swapped(jnp.concatenate([pieces, place, jnp.zeros_like(place)], axis=1))
    listed = came[:, Q, :TILES].astype(jnp.int32)
    own = (
        lax.axis_index("zh") * NP
        + (jnp.arange(NP) // ROWS * ROWS)[:, None]
        + jnp.arange(ROWS)[None, :]
    ).astype(jnp.int32)
    idx = jnp.concatenate([listed, own], axis=1).reshape(NP * WANT)

    def exchanged(mine):
        table = lax.all_gather(mine, "zh").reshape(TABLE, Q, BS)
        got = swapped(select(idx, table).reshape(NP, WANT * Q, BS))
        return got.reshape(NP * WANT * Q, BS)

    def summed(sums):
        got = swapped(sums.reshape(NP, ROWS * Q, BS))
        got = got.reshape(GROUPS, ROWS, ROWS * Q, BS).sum(axis=1)
        return got.reshape(NP, Q, BS)

    xj, xi, sums = first_call(col, exchanged(came[:, :Q]), omega_tiles, omega_diag)
    tiles, diag = omega_tiles, omega_diag
    for sweep in range(ITERS):
        got = exchanged(summed(sums))
        if sweep < ITERS - 1:
            tiles, diag, sums = sweep_call(col, got, tiles, diag, xj, xi)
        else:
            tiles, diag = last_call(col, got, tiles, diag, xj, xi)
    return tiles, diag


def solution(mesh):
    fine = Mesh(mesh.devices.reshape(X, ZH, ZL, Y, CORE), ("x", "zh", "zl", "y", "k"))
    rows = ("x", "zh", "zl")
    in_specs = (
        P(rows, COL, None, None),
        P(rows + COL, None),
        P(rows + COL, None),
        P(rows, COL),
    )
    out_specs = (P(rows, COL, None, None), P(rows + COL, None))
    return jax.shard_map(
        on_device, mesh=fine, in_specs=in_specs, out_specs=out_specs, check_vma=False
    )
```

time: 779 us -> 285 us (0.37)
  waiting for transfers between devices: 620 us -> 37.6 us
  blocking collectives: 0 us -> 191 us
  local copies, waits for them, and re-layouts: 56.3 us -> 1.92 us
  starting transfers between devices: 56.4 us -> 21.7 us
  Pallas kernels: 0 us -> 29.4 us
  matrix products: 22.7 us -> 0 us
  between operations: 14.3 us -> 0.75 us
    all_to_all x4 -> x2, waiting for transfers between devices: 546 us -> 37.6 us  [swapped(): return lax.all_to_all(value, PEERS, split_axis=0, concat_axis=0, tiled=True)]
    all_to_all x0 -> x4, blocking collectives: none -> 112 us  [swapped(): return lax.all_to_all(value, PEERS, split_axis=0, concat_axis=0, tiled=True)]
    all_gather x0 -> x3, blocking collectives: none -> 79.5 us  [exchanged(): table = lax.all_gather(mine, 'zh').reshape(TABLE, Q, BS)]
    all_gather x2 -> x0, waiting for transfers between devices: 74 us -> none  [over_pieces(): tiles = lax.all_gather(value, axis)]
    all_to_all x4 -> x2, starting transfers between devices: 56.1 us -> 21.7 us  [swapped(): return lax.all_to_all(value, PEERS, split_axis=0, concat_axis=0, tiled=True)]
    pallas_call x0 -> x6, Pallas kernels: none -> 29.4 us  [the longest x3 11.4 us: select(): pl.pallas_call(lambda i, t, o: select_kernel(i, t, o, dests=dests), grid_...]
    dot_general x10 -> x0, matrix products: 22.7 us -> none  [the longest x2 9.13 us: on_device(): jnp.einsum('akn,asqn->askq', x_blocks, unpack_slots(returned), precision=...]
    gather x9 -> x0, local copies, waits for them, and re-layouts: 20.6 us -> none  [the longest x3 10.9 us: unpack_slots(): received[dest_slot].reshape((block_rows, slot_count) + received.shape[1:])]
  transfers between devices with their start and end apart: 6 -> 2, of which waited for: 6 -> 2; matrix products, arithmetic and copies ran while one was open for 2% -> 0% of each run, Pallas kernels for 0% -> 0%
where the time goes in v1:
time: 285 us; the launch traced here: 284 us
  blocking collectives  191 us (67%)
  waiting for transfers between devices  37.6 us (13%)
  Pallas kernels  29.4 us (10%)
  starting transfers between devices  21.7 us (8%)
    all_to_all x4, blocking collectives, swapped(): return lax.all_to_all(value, PEERS, split_axis=0, concat_axis=0, tiled=True)  112 us
    all_gather x3, blocking collectives, exchanged(): table = lax.all_gather(mine, 'zh').reshape(TABLE, Q, BS)  79.5 us
    all_to_all x2, waiting for transfers between devices, swapped(): return lax.all_to_all(value, PEERS, split_axis=0, concat_axis=0, tiled=True)  37.6 us
    all_to_all x2, starting transfers between devices, swapped(): return lax.all_to_all(value, PEERS, split_axis=0, concat_axis=0, tiled=True)  21.7 us
    pallas_call x3, Pallas kernels, select(): pl.pallas_call(lambda i, t, o: select_kernel(i, t, o, dests=dests), grid_...  11.4 us
    pallas_call x1, Pallas kernels, on_device(): tiles, diag, sums = sweep_call(col, got, tiles, diag, xj, xi)  7.57 us
  transfers between devices with their start and end apart: 2, of which 2 were waited for; matrix products, arithmetic and copies ran while one was open for 0% of the time, Pallas kernels for 0%

profile of v1, /device:TPU:1, one launch (start us, length us, event | category | flops | bytes accessed | tf_op | source)
XLA Modules:
  0.0 284.5 jit_solution(14981081831950247766)
XLA Ops:
  0.6 0.7 fusion.4
  1.3 0.1 copy.19
  1.4 0.1 reshape.76
  1.5 0.1 pad.9.clone
  1.6 0.9 maximum_maximum_fusion
  2.5 0.7 copy.20
  3.3 10.9 %all-to-all-start = ((f32[64,4,128]{2,1,0:T(4,128)}), f32[64,4,128]{2,1,0:T(4,128)S(1)}, u32[]{:S(2)}, u32[]{:S(2)}) async-start(f32[64,4,128]{2,1,0:T(4,128)} %copy.20), calls=%async_computation | async-start | bytes 262144 | tf_op jit(solution)/shard_map/all_to_all | solution.py:190
  14.2 0.1 iota_add_fusion
  14.3 8.5 %all-to-all-done = f32[64,4,128]{2,1,0:T(4,128)S(1)} async-done(((f32[64,4,128]{2,1,0:T(4,128)}), f32[64,4,128]{2,1,0:T(4,128)S(1)}, u32[]{:S(2)}, u32[]{:S(2)}) %all-to-all-start) | async-done | bytes 131104 | tf_op jit(solution)/shard_map/all_to_all | solution.py:190
  22.9 0.1 pad_add_fusion
  23.0 0.1 reshape.77.i
  23.1 30.8 %all-gather.t = f32[512,2,128]{2,1,0:T(2,128)S(1)} all-gather(f32[64,2,128]{2,1,0:T(2,128)S(1)} %slice.9), channel_id=2, replica_groups=mesh['x'=4,'zh'=8,'zl'=2,'y'=4,'k'=2] {'zh'}, dimensions={0}, use_global_device_ids=true | all-gather | bytes 589824 | tf_op jit(solution)/shard_map/all_gather | solution.py:212
  53.8 5.1 %shard_map.59 = f32[64,32,2,128]{3,2,1,0:T(2,128)} custom-call(s32[2048]{0:T(1024)S(1)} %reshape.77.i, f32[512,2,128]{2,1,0:T(2,128)S(1)} %all-gather.t), custom_call_target="tpu_custom_call" | custom-call | tf_op jit(solution)/shard_map/pallas_call | solution.py:68
  58.9 0.0 copy-start
  58.9 0.0 copy-start.1
  58.9 10.7 %all-to-all-start.1 = ((f32[64,64,128]{2,1,0:T(8,128)}), f32[64,64,128]{2,1,0:T(8,128)}, u32[]{:S(2)}, u32[]{:S(2)}) async-start(f32[64,64,128]{2,1,0:T(8,128)} %bitcast.5), calls=%async_computation.1 | async-start | bytes 4194304 | tf_op jit(solution)/shard_map/all_to_all | solution.py:190
  69.6 29.1 %all-to-all-done.1 = f32[64,64,128]{2,1,0:T(8,128)} async-done(((f32[64,64,128]{2,1,0:T(8,128)}), f32[64,64,128]{2,1,0:T(8,128)}, u32[]{:S(2)}, u32[]{:S(2)}) %all-to-all-start.1) | async-done | bytes 2097184 | tf_op jit(solution)/shard_map/all_to_all | solution.py:190
  98.7 0.0 copy-done
  98.7 0.0 copy-done.1
  98.7 5.2 %shard_map.60 = (bf16[2,24,128,128]{3,2,1,0:T(8,128)(2,1)S(1)}, bf16[2,8,128,128]{3,2,1,0:T(8,128)(2,1)S(1)}, f32[1024,128]{1,0:T(8,128)S(1)}) custom-call(s32[1]{0:T(128)} %bitcast.col, f32[4096,128]{1,0:T(8,128)} %bitcast.6.recv, f32[8,3,128,128]{3,2,1,0:T(8,128)S(1)} %copy-done, f32[128,128]{1,0:T(8,128)S(1)} %copy-done.1), custom_call_target="tpu_custom_call" | custom-call | tf_op jit(solution)/shard_map/pallas_call | solution.py:221
  103.9 16.9 %all_to_all.30 = f32[64,16,128]{2,1,0:T(8,128)S(1)} all-to-all(f32[64,16,128]{2,1,0:T(8,128)S(1)} %bitcast.29), channel_id=1, replica_groups=mesh['x'=4,'zh'=8,'zl'=2,'y'=4,'k'=2] {'x','zl','y','k'}, dimensions={0} | all-to-all | bytes 1048576 | tf_op jit(solution)/shard_map/all_to_all | solution.py:190
  120.9 24.6 %all_gather.14 = f32[8,64,2,128]{3,1,2,0:T(8,128)S(1)} all-gather(f32[1,64,2,128]{3,1,2,0:T(8,128)S(1)} %copy.21), channel_id=1, replica_groups=mesh['x'=4,'zh'=8,'zl'=2,'y'=4,'k'=2] {'zh'}, dimensions={0}, use_global_device_ids=true | all-gather | bytes 589824 | tf_op jit(solution)/shard_map/all_gather | solution.py:212
  145.4 0.4 copy.22
  145.8 3.2 %shard_map.61 = f32[64,32,2,128]{3,2,1,0:T(2,128)S(1)} custom-call(s32[2048]{0:T(1024)S(1)} %reshape.77.i, f32[512,2,128]{2,1,0:T(2,128)S(1)} %bitcast.28), custom_call_target="tpu_custom_call" | custom-call | tf_op jit(solution)/shard_map/pallas_call | solution.py:68
  149.0 39.0 %all_to_all.31 = f32[64,64,128]{2,1,0:T(8,128)} all-to-all(f32[64,64,128]{2,1,0:T(8,128)S(1)} %bitcast.26), channel_id=1, replica_groups=mesh['x'=4,'zh'=8,'zl'=2,'y'=4,'k'=2] {'x','zl','y','k'}, dimensions={0} | all-to-all | bytes 4194304 | tf_op jit(solution)/shard_map/all_to_all | solution.py:190
  188.0 7.6 %shard_map.62 = (f32[8,3,128,128]{3,2,1,0:T(8,128)S(1)}, f32[128,128]{1,0:T(8,128)S(1)}, f32[1024,128]{1,0:T(8,128)S(1)}) custom-call(s32[1]{0:T(128)} %bitcast.col, f32[4096,128]{1,0:T(8,128)} %bitcast.31, f32[8,3,128,128]{3,2,1,0:T(8,128)S(1)} %copy-done, f32[128,128]{1,0:T(8,128)S(1)} %copy-done.1, bf16[2,24,128,128]{3,2,1,0:T(8,128)(2,1)S(1)} %get-tuple-element.9.xj, ...), custom_call_target="tpu_custom_call" | custom-call | tf_op jit(solution)/shard_map/pallas_call | solution.py:226
  195.5 16.9 %all_to_all.32 = f32[64,16,128]{2,1,0:T(8,128)S(1)} all-to-all(f32[64,16,128]{2,1,0:T(8,128)S(1)} %bitcast.30), channel_id=1, replica_groups=mesh['x'=4,'zh'=8,'zl'=2,'y'=4,'k'=2] {'x','zl','y','k'}, dimensions={0} | all-to-all | bytes 1048576 | tf_op jit(solution)/shard_map/all_to_all | solution.py:190
  212.5 24.2 %all_gather.15 = f32[8,64,2,128]{3,1,2,0:T(8,128)S(1)} all-gather(f32[1,64,2,128]{3,1,2,0:T(8,128)S(1)} %copy.23), channel_id=1, replica_groups=mesh['x'=4,'zh'=8,'zl'=2,'y'=4,'k'=2] {'zh'}, dimensions={0}, use_global_device_ids=true | all-gather | bytes 589824 | tf_op jit(solution)/shard_map/all_gather | solution.py:212
  236.7 0.4 copy.24
  237.2 3.2 %shard_map.63 = f32[64,32,2,128]{3,2,1,0:T(2,128)S(1)} custom-call(s32[2048]{0:T(1024)S(1)} %reshape.77.i, f32[512,2,128]{2,1,0:T(2,128)S(1)} %bitcast.27), custom_call_target="tpu_custom_call" | custom-call | tf_op jit(solution)/shard_map/pallas_call | solution.py:68
  240.3 38.9 %all_to_all.33 = f32[64,64,128]{2,1,0:T(8,128)S(1)} all-to-all(f32[64,64,128]{2,1,0:T(8,128)S(1)} %bitcast.25), channel_id=1, replica_groups=mesh['x'=4,'zh'=8,'zl'=2,'y'=4,'k'=2] {'x','zl','y','k'}, dimensions={0} | all-to-all | bytes 4194304 | tf_op jit(solution)/shard_map/all_to_all | solution.py:190
  279.3 5.2 %shard_map.64 = (f32[8,3,128,128]{3,2,1,0:T(8,128)}, f32[128,128]{1,0:T(8,128)}) custom-call(s32[1]{0:T(128)} %bitcast.col, f32[4096,128]{1,0:T(8,128)S(1)} %bitcast.24, f32[8,3,128,128]{3,2,1,0:T(8,128)S(1)} %get-tuple-element.12.tiles, f32[128,128]{1,0:T(8,128)S(1)} %get-tuple-element.13.diag, bf16[2,24,128,128]{3,2,1,0:T(8,128)(2,1)S(1)} %get-tuple-element.9.xj, ...), custom_call_target="tpu_custom_call" | custom-call | tf_op jit(solution)/shard_map/pallas_call | solution.py:228
  (9 shorter events, 0.2 us)
Async XLA Ops:
  3.3 19.6 %all-to-all-start = ((f32[64,4,128]{2,1,0:T(4,128)}), f32[64,4,128]{2,1,0:T(4,128)S(1)}, u32[]{:S(2)}, u32[]{:S(2)}) async-start(f32[64,4,128]{2,1,0:T(4,128)} %copy.20), calls=%async_computation | async-start | bytes 262144 | tf_op jit(solution)/shard_map/all_to_all | solution.py:190
  58.9 39.8 %copy-start = (f32[8,3,128,128]{3,2,1,0:T(8,128)S(1)}, f32[8,3,128,128]{3,2,1,0:T(8,128)}, u32[]{:S(2)}) copy-start(f32[8,3,128,128]{3,2,1,0:T(8,128)} %tiles.3) | copy-start | bytes 4718596
  58.9 39.8 %copy-start.1 = (f32[128,128]{1,0:T(8,128)S(1)}, f32[128,128]{1,0:T(8,128)}, u32[]{:S(2)}) copy-start(f32[128,128]{1,0:T(8,128)} %diag.3) | copy-start | bytes 196612
  58.9 39.8 %all-to-all-start.1 = ((f32[64,64,128]{2,1,0:T(8,128)}), f32[64,64,128]{2,1,0:T(8,128)}, u32[]{:S(2)}, u32[]{:S(2)}) async-start(f32[64,64,128]{2,1,0:T(8,128)} %bitcast.5), calls=%async_computation.1 | async-start | bytes 4194304 | tf_op jit(solution)/shard_map/all_to_all | solution.py:190

commit v2 on v1

v2 whole, which is shorter than its diff:
```python
import jax
import jax.numpy as jnp
from jax import lax
from jax.experimental import pallas as pl
from jax.experimental.pallas import tpu as pltpu
from jax.sharding import Mesh
from jax.sharding import PartitionSpec as P

ITERS = 2
STEP = 0.2
SHRINK = 0.05
RIDGE = 0.1

BS = 128
ROWS = 8
SLOTS = 3
TILES = ROWS * SLOTS
WANT = TILES + ROWS

X, Z, Y, CORE = 4, 16, 4, 2
ZL = 2
ZH = Z // ZL
COL = ("y", "k")
PEERS = ("x", "zl", "y", "k")
NP = X * ZL * Y * CORE
Q = BS // NP
GROUPS = NP // ROWS
TABLE = ZH * NP
PITCH = NP + 8
SENT = 4

VMEM = 48 * 1024 * 1024


def split(v):
    hi = v.astype(jnp.bfloat16)
    lo = (v - hi.astype(jnp.float32)).astype(jnp.bfloat16)
    return hi, lo


def dot(a, b, rhs_dim):
    return lax.dot_general(
        a, b, (((1,), (rhs_dim,)), ((), ())), preferred_element_type=jnp.float32
    )


def shrink(v):
    t = STEP * SHRINK
    return v - jnp.clip(v, -t, t)


def send_kernel(pattern, samples, out):
    for q in range(Q):
        out[pl.ds(q, NP, stride=SENT), :] = samples[q * NP : (q + 1) * NP]
    lane = lax.broadcasted_iota(jnp.int32, (1, BS), 1)
    listed = jnp.zeros((1, BS), jnp.int32)
    for i in range(ROWS):
        for s in range(SLOTS):
            listed = jnp.where(lane == i * SLOTS + s, pattern[s, i], listed)
    listed = jnp.broadcast_to(listed.astype(jnp.float32), (NP, BS))
    for q in range(Q, SENT):
        out[pl.ds(q, NP, stride=SENT), :] = listed


def select_kernel(place, plane, table, out):
    def one(d, carry):
        for t in range(TILES):
            out[d, t] = table[place[d * TILES + t]]
        out[d, TILES:] = table[pl.ds(plane[0] * NP + d // ROWS * ROWS, ROWS)]
        return carry

    lax.fori_loop(0, NP, one, 0, unroll=2)


def reorder(recv, blocks):
    def one(p, carry):
        for w in range(0, WANT * Q, 8):
            part = recv[pl.ds(pl.multiple_of(p * WANT * Q, 8) + w, 8), :]
            blocks[pl.ds(w * PITCH + p, 8, stride=PITCH), :] = part
        return carry

    lax.fori_loop(0, NP, one, 0, unroll=4)


def assembled(blocks, t):
    parts = []
    for q in range(Q):
        start = pl.multiple_of((t * Q + q) * PITCH, 8)
        parts.append(blocks[pl.ds(start, NP), :])
    return jnp.concatenate(parts, axis=0)


def spread(out, i, value):
    for q in range(Q):
        out[pl.ds(i * Q + q, NP, stride=ROWS * Q), :] = value[q * NP : (q + 1) * NP]


def lhs3(pairs):
    return jnp.concatenate([p[n] for n in (0, 0, 1) for p in pairs], axis=1)


def rhs3(pairs, axis):
    return jnp.concatenate([p[n] for n in (0, 1, 0) for p in pairs], axis=axis)


def spread_more(out, i, value):
    for q in range(Q):
        rows = pl.ds(i * Q + q, NP, stride=ROWS * Q)
        out[rows, :] = out[rows, :] + value[q * NP : (q + 1) * NP]


def first_kernel(col, recv, tiles, diag, xj, xi, sums, blocks):
    reorder(recv, blocks)

    def one(i, carry):
        xs = []
        for s in range(SLOTS):
            x = split(assembled(blocks, i * SLOTS + s))
            xs.append(x)
            xj[0, i * SLOTS + s], xj[1, i * SLOTS + s] = x
        xi[0, i], xi[1, i] = split(assembled(blocks, TILES + i))
        bs = [split(tiles[i, s]) for s in range(SLOTS)]
        spread(sums, i, dot(lhs3(bs), rhs3(xs, 0), 0))
        return carry

    lax.fori_loop(0, ROWS, one, 0, unroll=2)
    c = col[0]
    own = (xi[0, c], xi[1, c])
    spread_more(sums, c, dot(lhs3([split(diag[...])]), rhs3([own], 0), 0))


def sweep_kernel(col, recv, tiles, diag, xj, xi, new_tiles, new_diag, *rest):
    *rest, blocks = rest
    reorder(recv, blocks)

    def one(i, carry):
        own_x = (xi[0, i], xi[1, i])
        own_y = split(assembled(blocks, TILES + i))
        lhs = lhs3([own_y, own_x])
        xs = [(xj[0, i * SLOTS + s], xj[1, i * SLOTS + s]) for s in range(SLOTS)]
        ys = [split(assembled(blocks, i * SLOTS + s)) for s in range(SLOTS)]
        rhs = [rhs3([x, y], 1) for x, y in zip(xs, ys)]
        cross = dot(lhs, jnp.concatenate(rhs, axis=0), 1)
        bs = []
        for s in range(SLOTS):
            old = tiles[i, s]
            part = cross[:, s * BS : (s + 1) * BS]
            new = shrink(old - STEP * (part * (0.5 / BS) + RIDGE * old))
            new_tiles[i, s] = new
            bs.append(split(new) if rest else None)
        if rest:
            spread(rest[0], i, dot(lhs3(bs), rhs3(xs, 0), 0))
        return carry

    lax.fori_loop(0, ROWS, one, 0, unroll=ROWS if rest else 2)
    c = col[0]
    own_x = (xi[0, c], xi[1, c])
    own_y = split(assembled(blocks, TILES + c))
    cross = dot(lhs3([own_y, own_x]), rhs3([own_x, own_y], 1), 1)
    old = diag[...]
    shape = (BS, BS)
    eye = lax.broadcasted_iota(jnp.int32, shape, 0) == lax.broadcasted_iota(
        jnp.int32, shape, 1
    )
    pivots = jnp.where(eye, 1.0 / jnp.where(eye, old, 1.0), 0.0)
    stepped = old - STEP * (cross * (0.5 / BS) + RIDGE * old - pivots)
    new = jnp.where(eye, stepped, shrink(stepped))
    new_diag[...] = new
    if rest:
        spread_more(rest[0], c, dot(lhs3([split(new)]), rhs3([own_x], 0), 0))


in_smem = pl.BlockSpec(memory_space=pltpu.SMEM)
in_vmem = pl.BlockSpec(memory_space=pltpu.VMEM)
FLOAT, HALF = jnp.float32, jnp.bfloat16
TABLE_SHAPE = (TABLE, Q, BS)
BLOCKS = pltpu.VMEM((WANT * Q * PITCH, BS), FLOAT)


def call(kernel, scalars, arrays, outputs, scratch=()):
    shapes = [jax.ShapeDtypeStruct(o, t) for o, t in outputs]
    several = len(shapes) > 1
    return pl.pallas_call(
        kernel,
        in_specs=[in_smem] * scalars + [in_vmem] * arrays,
        out_specs=[in_vmem] * len(shapes) if several else in_vmem,
        out_shape=shapes if several else shapes[0],
        scratch_shapes=scratch,
        compiler_params=pltpu.CompilerParams(vmem_limit_bytes=VMEM),
    )


send = call(send_kernel, 1, 1, [((NP * SENT, BS), FLOAT)])
select = call(select_kernel, 2, 1, [((NP, WANT, Q, BS), FLOAT)])
xs_out = [((2, TILES, BS, BS), HALF), ((2, ROWS, BS, BS), HALF)]
new_out = [((ROWS, SLOTS, BS, BS), FLOAT), ((BS, BS), FLOAT)]
sums_out = [((NP * ROWS * Q, BS), FLOAT)]
first_call = call(first_kernel, 1, 3, xs_out + sums_out, [BLOCKS])
sweep_call = call(sweep_kernel, 1, 5, new_out + sums_out, [BLOCKS])
last_call = call(sweep_kernel, 1, 5, new_out, [BLOCKS])


def swapped(value, rows):
    return lax.all_to_all(
        value.reshape(NP, rows, BS), PEERS, split_axis=0, concat_axis=0, tiled=True
    )


def on_device(omega_tiles, omega_diag, samples, pattern):
    col = lax.axis_index(COL).astype(jnp.int32).reshape(1)
    plane = lax.axis_index("zh").astype(jnp.int32).reshape(1)
    came = swapped(send(pattern.T, samples), SENT)
    block = came[:, Q, :TILES].astype(jnp.int32)
    row, member = block // ROWS, block % ROWS
    place = (row % Z) // ZL * NP + (row // Z * ZL + row % ZL) * ROWS + member
    place = place.reshape(NP * TILES)

    def exchanged(mine):
        table = lax.all_gather(mine, "zh").reshape(TABLE_SHAPE)
        got = swapped(select(place, plane, table), WANT * Q)
        return got.reshape(NP * WANT * Q, BS)

    got = exchanged(came[:, :Q].reshape(NP * Q, BS))
    xj, xi, sums = first_call(col, got, omega_tiles, omega_diag)
    tiles, diag = omega_tiles, omega_diag
    for sweep in range(ITERS):
        parts = swapped(sums, ROWS * Q).reshape(GROUPS, ROWS, ROWS * Q, BS)
        got = exchanged(parts.sum(axis=1).reshape(NP * Q, BS))
        if sweep < ITERS - 1:
            tiles, diag, sums = sweep_call(col, got, tiles, diag, xj, xi)
        else:
            tiles, diag = last_call(col, got, tiles, diag, xj, xi)
    return tiles, diag


def solution(mesh):
    fine = Mesh(mesh.devices.reshape(X, ZH, ZL, Y, CORE), ("x", "zh", "zl", "y", "k"))
    rows = ("x", "zh", "zl")
    in_specs = (
        P(rows, COL, None, None),
        P(rows + COL, None),
        P(rows + COL, None),
        P(rows, COL),
    )
    out_specs = (P(rows, COL, None, None), P(rows + COL, None))
    return jax.shard_map(
        on_device, mesh=fine, in_specs=in_specs, out_specs=out_specs, check_vma=False
    )
```

time: 285 us -> 277 us (0.972)
  Pallas kernels: 29.4 us -> 23.5 us
    pallas_call x4 -> x5, Pallas kernels: 16.6 us -> 14.6 us  [the longest x3 9.6 us: exchanged(): got = swapped(select(place, plane, table), WANT * Q)]
where the time goes in v2:
time: 277 us
  blocking collectives  191 us (69%)
  waiting for transfers between devices  37.7 us (14%)
  Pallas kernels  23.5 us (8%)
  starting transfers between devices  21.7 us (8%)
    all_to_all x4, blocking collectives, swapped(): lax.all_to_all(value.reshape(NP, rows, BS), PEERS, split_axis=0, concat_a...  111 us
    all_gather x3, blocking collectives, exchanged(): table = lax.all_gather(mine, 'zh').reshape(TABLE_SHAPE)  80.1 us
    all_to_all x2, waiting for transfers between devices, swapped(): lax.all_to_all(value.reshape(NP, rows, BS), PEERS, split_axis=0, concat_a...  37.7 us
    all_to_all x2, starting transfers between devices, swapped(): lax.all_to_all(value.reshape(NP, rows, BS), PEERS, split_axis=0, concat_a...  21.7 us
    pallas_call x3, Pallas kernels, exchanged(): got = swapped(select(place, plane, table), WANT * Q)  9.6 us
  transfers between devices with their start and end apart: 2, of which 2 were waited for; matrix products, arithmetic and copies ran while one was open for 0% of the time, Pallas kernels for 0%

profile of v2, /device:TPU:1, one launch (start us, length us, event | category | flops | bytes accessed | tf_op | source)
XLA Modules:
  0.0 276.8 jit_solution(9301429817339567514)
XLA Ops:
  0.6 0.0 copy-start.2
  0.6 0.8 copy-done.2
  1.5 0.0 copy-start.3
  1.5 0.7 copy-done.3
  2.2 1.2 shard_map.59
  3.4 10.9 %all-to-all-start = ((f32[64,4,128]{2,1,0:T(4,128)}), f32[64,4,128]{2,1,0:T(4,128)S(1)}, u32[]{:S(2)}, u32[]{:S(2)}) async-start(f32[64,4,128]{2,1,0:T(4,128)} %bitcast.2), calls=%async_computation | async-start | bytes 262144 | tf_op jit(solution)/shard_map/all_to_all | solution.py:204
  14.3 8.6 %all-to-all-done = f32[64,4,128]{2,1,0:T(4,128)S(1)} async-done(((f32[64,4,128]{2,1,0:T(4,128)}), f32[64,4,128]{2,1,0:T(4,128)S(1)}, u32[]{:S(2)}, u32[]{:S(2)}) %all-to-all-start) | async-done | bytes 131104 | tf_op jit(solution)/shard_map/all_to_all | solution.py:204
  23.0 0.1 fusion
  23.1 0.1 convert_element_type.8
  23.3 30.8 %all_gather.9 = f32[8,128,128]{2,1,0:T(8,128)S(1)} all-gather(f32[1,128,128]{2,1,0:T(8,128)S(1)} %bitcast.34), channel_id=1, replica_groups=mesh['x'=4,'zh'=8,'zl'=2,'y'=4,'k'=2] {'zh'}, dimensions={0}, use_global_device_ids=true | all-gather | bytes 589824 | tf_op jit(solution)/shard_map/all_gather | solution.py:219
  54.0 4.1 %shard_map.60 = f32[64,32,2,128]{3,2,1,0:T(2,128)} custom-call(s32[1536]{0:T(1024)S(1)} %fusion.4.place, s32[1]{0:T(128)} %bitcast.3.plane, f32[512,2,128]{2,1,0:T(2,128)S(1)} %bitcast.26), custom_call_target="tpu_custom_call" | custom-call | tf_op jit(solution)/shard_map/pallas_call | solution.py:220
  58.1 0.0 copy-start
  58.1 0.0 copy-start.1
  58.1 10.7 %all-to-all-start.1 = ((f32[64,64,128]{2,1,0:T(8,128)}), f32[64,64,128]{2,1,0:T(8,128)}, u32[]{:S(2)}, u32[]{:S(2)}) async-start(f32[64,64,128]{2,1,0:T(8,128)} %bitcast.6), calls=%async_computation.1 | async-start | bytes 4194304 | tf_op jit(solution)/shard_map/all_to_all | solution.py:204
  68.8 29.1 %all-to-all-done.1 = f32[64,64,128]{2,1,0:T(8,128)} async-done(((f32[64,64,128]{2,1,0:T(8,128)}), f32[64,64,128]{2,1,0:T(8,128)}, u32[]{:S(2)}, u32[]{:S(2)}) %all-to-all-start.1) | async-done | bytes 2097184 | tf_op jit(solution)/shard_map/all_to_all | solution.py:204
  97.9 0.0 copy-done
  97.9 0.0 copy-done.1
  97.9 3.7 %shard_map.61 = (bf16[2,24,128,128]{3,2,1,0:T(8,128)(2,1)S(1)}, bf16[2,8,128,128]{3,2,1,0:T(8,128)(2,1)S(1)}, f32[1024,128]{1,0:T(8,128)S(1)}) custom-call(s32[1]{0:T(128)} %bitcast.col, f32[4096,128]{1,0:T(8,128)} %bitcast.7.recv, f32[8,3,128,128]{3,2,1,0:T(8,128)S(1)} %copy-done, f32[128,128]{1,0:T(8,128)S(1)} %copy-done.1), custom_call_target="tpu_custom_call" | custom-call | tf_op jit(solution)/shard_map/pallas_call | solution.py:224
  101.6 16.9 %all_to_all.30 = f32[64,16,128]{2,1,0:T(8,128)S(1)} all-to-all(f32[64,16,128]{2,1,0:T(8,128)S(1)} %bitcast.28), channel_id=1, replica_groups=mesh['x'=4,'zh'=8,'zl'=2,'y'=4,'k'=2] {'x','zl','y','k'}, dimensions={0} | all-to-all | bytes 1048576 | tf_op jit(solution)/shard_map/all_to_all | solution.py:204
  118.6 25.0 %all_gather.10 = f32[8,128,128]{2,1,0:T(8,128)S(1)} all-gather(f32[1,128,128]{2,1,0:T(8,128)S(1)} %bitcast.32), channel_id=1, replica_groups=mesh['x'=4,'zh'=8,'zl'=2,'y'=4,'k'=2] {'zh'}, dimensions={0}, use_global_device_ids=true | all-gather | bytes 589824 | tf_op jit(solution)/shard_map/all_gather | solution.py:219
  143.6 2.8 shard_map.62
  146.4 38.5 %all_to_all.31 = f32[64,64,128]{2,1,0:T(8,128)} all-to-all(f32[64,64,128]{2,1,0:T(8,128)S(1)} %bitcast.24), channel_id=1, replica_groups=mesh['x'=4,'zh'=8,'zl'=2,'y'=4,'k'=2] {'x','zl','y','k'}, dimensions={0} | all-to-all | bytes 4194304 | tf_op jit(solution)/shard_map/all_to_all | solution.py:204
  184.9 5.4 %shard_map.63 = (f32[8,3,128,128]{3,2,1,0:T(8,128)S(1)}, f32[128,128]{1,0:T(8,128)S(1)}, f32[1024,128]{1,0:T(8,128)S(1)}) custom-call(s32[1]{0:T(128)} %bitcast.col, f32[4096,128]{1,0:T(8,128)} %bitcast.31, f32[8,3,128,128]{3,2,1,0:T(8,128)S(1)} %copy-done, f32[128,128]{1,0:T(8,128)S(1)} %copy-done.1, bf16[2,24,128,128]{3,2,1,0:T(8,128)(2,1)S(1)} %get-tuple-element.9.xj, ...), custom_call_target="tpu_custom_call" | custom-call | tf_op jit(solution)/shard_map/pallas_call | solution.py:230
  190.3 16.9 %all_to_all.32 = f32[64,16,128]{2,1,0:T(8,128)S(1)} all-to-all(f32[64,16,128]{2,1,0:T(8,128)S(1)} %bitcast.29), channel_id=1, replica_groups=mesh['x'=4,'zh'=8,'zl'=2,'y'=4,'k'=2] {'x','zl','y','k'}, dimensions={0} | all-to-all | bytes 1048576 | tf_op jit(solution)/shard_map/all_to_all | solution.py:204
  207.2 24.3 %all_gather.11 = f32[8,128,128]{2,1,0:T(8,128)S(1)} all-gather(f32[1,128,128]{2,1,0:T(8,128)S(1)} %bitcast.33), channel_id=1, replica_groups=mesh['x'=4,'zh'=8,'zl'=2,'y'=4,'k'=2] {'zh'}, dimensions={0}, use_global_device_ids=true | all-gather | bytes 589824 | tf_op jit(solution)/shard_map/all_gather | solution.py:219
  231.5 2.8 shard_map.64
  234.3 38.9 %all_to_all.33 = f32[64,64,128]{2,1,0:T(8,128)S(1)} all-to-all(f32[64,64,128]{2,1,0:T(8,128)S(1)} %bitcast.23), channel_id=1, replica_groups=mesh['x'=4,'zh'=8,'zl'=2,'y'=4,'k'=2] {'x','zl','y','k'}, dimensions={0} | all-to-all | bytes 4194304 | tf_op jit(solution)/shard_map/all_to_all | solution.py:204
  273.2 3.6 %shard_map.65 = (f32[8,3,128,128]{3,2,1,0:T(8,128)}, f32[128,128]{1,0:T(8,128)}) custom-call(s32[1]{0:T(128)} %bitcast.col, f32[4096,128]{1,0:T(8,128)S(1)} %bitcast.22, f32[8,3,128,128]{3,2,1,0:T(8,128)S(1)} %get-tuple-element.12.tiles, f32[128,128]{1,0:T(8,128)S(1)} %get-tuple-element.13.diag, bf16[2,24,128,128]{3,2,1,0:T(8,128)(2,1)S(1)} %get-tuple-element.9.xj, ...), custom_call_target="tpu_custom_call" | custom-call | tf_op jit(solution)/shard_map/pallas_call | solution.py:232
  (4 shorter events, 0.1 us)
Async XLA Ops:
  0.6 0.8 copy-start.2
  1.5 0.7 copy-start.3
  3.4 19.6 %all-to-all-start = ((f32[64,4,128]{2,1,0:T(4,128)}), f32[64,4,128]{2,1,0:T(4,128)S(1)}, u32[]{:S(2)}, u32[]{:S(2)}) async-start(f32[64,4,128]{2,1,0:T(4,128)} %bitcast.2), calls=%async_computation | async-start | bytes 262144 | tf_op jit(solution)/shard_map/all_to_all | solution.py:204
  58.1 39.8 %copy-start = (f32[8,3,128,128]{3,2,1,0:T(8,128)S(1)}, f32[8,3,128,128]{3,2,1,0:T(8,128)}, u32[]{:S(2)}) copy-start(f32[8,3,128,128]{3,2,1,0:T(8,128)} %tiles.3) | copy-start | bytes 4718596
  58.1 39.8 %copy-start.1 = (f32[128,128]{1,0:T(8,128)S(1)}, f32[128,128]{1,0:T(8,128)}, u32[]{:S(2)}) copy-start(f32[128,128]{1,0:T(8,128)} %diag.3) | copy-start | bytes 196612
  58.1 39.8 %all-to-all-start.1 = ((f32[64,64,128]{2,1,0:T(8,128)}), f32[64,64,128]{2,1,0:T(8,128)}, u32[]{:S(2)}, u32[]{:S(2)}) async-start(f32[64,64,128]{2,1,0:T(8,128)} %bitcast.6), calls=%async_computation.1 | async-start | bytes 4194304 | tf_op jit(solution)/shard_map/all_to_all | solution.py:204

commit v3 on v2

v3 whole, which is shorter than its diff:
```python
import functools

import jax
import jax.numpy as jnp
from jax import lax
from jax.experimental import pallas as pl
from jax.experimental.pallas import tpu as pltpu
from jax.sharding import Mesh
from jax.sharding import PartitionSpec as P

ITERS = 2
STEP = 0.2
SHRINK = 0.05
RIDGE = 0.1

BS = 128
ROWS = 8
SLOTS = 3
TILES = ROWS * SLOTS
OWN = ROWS // 2
WIDE = 2 * SLOTS
WANT = TILES + OWN

X, Z, Y, CORE = 4, 16, 4, 2
ZL = 2
ZH = Z // ZL
COL = ("y", "k")
PEERS = ("x", "zl", "k", "y")
NP = X * ZL * Y * CORE
Q = BS // NP
GROUPS = NP // ROWS
TABLE = ZH * NP
PITCH = NP + 8
SENT = 4

VMEM = 48 * 1024 * 1024


def split(v):
    hi = v.astype(jnp.bfloat16)
    lo = (v - hi.astype(jnp.float32)).astype(jnp.bfloat16)
    return hi, lo


def dot(a, b, rhs_dim):
    return lax.dot_general(
        a, b, (((1,), (rhs_dim,)), ((), ())), preferred_element_type=jnp.float32
    )


def turned(member):
    return member % CORE * Y + member // CORE


def shrink(v):
    t = STEP * SHRINK
    return v - jnp.clip(v, -t, t)


def send_kernel(pattern, samples, out, numbers, block, sems):
    copies = loading([samples, pattern], [block, numbers], sems)
    copies[0].wait()
    for q in range(Q):
        out[pl.ds(q, NP, stride=SENT), :] = block[q * NP : (q + 1) * NP]
    copies[1].wait()
    lane = lax.broadcasted_iota(jnp.int32, (1, BS), 1)
    listed = jnp.zeros((1, BS), jnp.int32)
    for i in range(ROWS):
        for s in range(SLOTS):
            listed = jnp.where(lane == i * SLOTS + s, numbers[s, i], listed)
    listed = jnp.broadcast_to(listed.astype(jnp.float32), (NP, BS))
    for q in range(Q, SENT):
        out[pl.ds(q, NP, stride=SENT), :] = listed


def select_kernel(place, plane, table, out, numbers, sems):
    [copy] = loading([place], [numbers], sems)

    def rows(d, carry):
        out[d, TILES:] = table[pl.ds(plane[0] * NP + d // OWN * OWN, OWN)]
        return carry

    lax.fori_loop(0, NP, rows, 0, unroll=4)
    copy.wait()

    def columns(n, carry):
        pair = n // Y * ROWS + n % Y
        pair = (pair, pair + Y)
        bases = [peer * TILES for peer in pair]
        for core in range(CORE):
            for t in range(TILES):
                base = bases[core ^ t % WIDE // SLOTS]
                entry = t // WIDE * CORE * SLOTS + core * SLOTS + t % SLOTS
                out[pair[core], t] = table[numbers[base + entry]]
        return carry

    lax.fori_loop(0, NP // CORE, columns, 0)


def loading(sources, places, sems):
    copies = []
    for n, (source, place) in enumerate(zip(sources, places)):
        copies.append(pltpu.make_async_copy(source, place, sems.at[n]))
        copies[n].start()
    return copies


def reorder(recv, blocks):
    def one(p, carry):
        for w in range(0, WANT * Q, 8):
            part = recv[pl.ds(pl.multiple_of(p * WANT * Q, 8) + w, 8), :]
            blocks[pl.ds(w * PITCH + p, 8, stride=PITCH), :] = part
        return carry

    lax.fori_loop(0, NP, one, 0, unroll=4)


def assembled(blocks, t):
    parts = []
    for q in range(Q):
        start = pl.multiple_of((t * Q + q) * PITCH, 8)
        parts.append(blocks[pl.ds(start, NP), :])
    return jnp.concatenate(parts, axis=0)


def spread(out, i, value, add=False):
    each = out.shape[0] // NP
    for q in range(Q):
        rows = pl.ds(i * Q + q, NP, stride=each)
        part = value[q * NP : (q + 1) * NP]
        out[rows, :] = out[rows, :] + part if add else part


def lhs3(pairs):
    return jnp.concatenate([p[n] for n in (0, 0, 1) for p in pairs], axis=1)


def rhs3(pairs, axis):
    return jnp.concatenate([p[n] for n in (0, 1, 0) for p in pairs], axis=axis)


def first_kernel(at, recv, tiles, other, diag, xj, xi, held, sums, blocks):
    reorder(recv, blocks)

    def one(i, carry):
        xs, bs = [], []
        for s in range(WIDE):
            x = split(assembled(blocks, i * WIDE + s))
            xs.append(x)
            xj[0, i * WIDE + s], xj[1, i * WIDE + s] = x
            b = tiles[i * CORE + at[0], s] if s < SLOTS else other[i, s - SLOTS]
            held[i, s] = b
            bs.append(split(b))
        xi[0, i], xi[1, i] = split(assembled(blocks, TILES + i))
        spread(sums, i, dot(lhs3(bs), rhs3(xs, 0), 0))
        return carry

    lax.fori_loop(0, OWN, one, 0, unroll=FIRST_UNROLL)
    c = at[1]
    own = (xi[0, c], xi[1, c])
    spread(sums, c, dot(lhs3([split(diag[...])]), rhs3([own], 0), 0), add=True)


def sweep_kernel(last, at, recv, tiles, diag, xj, xi, *rest):
    *new_tiles, new_diag, sums, blocks = rest if not last else (*rest[:-1], None, rest[-1])
    reorder(recv, blocks)

    def one(i, carry):
        own_x = (xi[0, i], xi[1, i])
        own_y = split(assembled(blocks, TILES + i))
        lhs = lhs3([own_y, own_x])
        bs, xs = [], []
        for half in range(2):
            at_half = range(half * SLOTS, (half + 1) * SLOTS)
            half_xs = [(xj[0, i * WIDE + s], xj[1, i * WIDE + s]) for s in at_half]
            ys = [split(assembled(blocks, i * WIDE + s)) for s in at_half]
            rhs = [rhs3([x, y], 1) for x, y in zip(half_xs, ys)]
            cross = dot(lhs, jnp.concatenate(rhs, axis=0), 1)
            xs += half_xs
            for n, s in enumerate(at_half):
                old = tiles[i, s]
                part = cross[:, n * BS : (n + 1) * BS]
                new = shrink(old - STEP * (part * (0.5 / BS) + RIDGE * old))
                if last:
                    new_tiles[half][i, n] = new
                else:
                    new_tiles[0][i, s] = new
                    bs.append(split(new))
        if not last:
            spread(sums, i, dot(lhs3(bs), rhs3(xs, 0), 0))
        return carry

    lax.fori_loop(0, OWN, one, 0, unroll=OWN)
    c = at[1]
    own_x = (xi[0, c], xi[1, c])
    own_y = split(assembled(blocks, TILES + c))
    cross = dot(lhs3([own_y, own_x]), rhs3([own_x, own_y], 1), 1)
    old = diag[...]
    shape = (BS, BS)
    eye = lax.broadcasted_iota(jnp.int32, shape, 0) == lax.broadcasted_iota(
        jnp.int32, shape, 1
    )
    pivots = jnp.where(eye, 1.0 / jnp.where(eye, old, 1.0), 0.0)
    stepped = old - STEP * (cross * (0.5 / BS) + RIDGE * old - pivots)
    new = jnp.where(eye, stepped, shrink(stepped))
    new_diag[...] = new
    if not last:
        spread(sums, c, dot(lhs3([split(new)]), rhs3([own_x], 0), 0), add=True)


FIRST_UNROLL = 2
SPACES = {
    "s": pl.BlockSpec(memory_space=pltpu.SMEM),
    "v": pl.BlockSpec(memory_space=pltpu.VMEM),
    "a": pl.BlockSpec(memory_space=pl.ANY),
}
FLOAT, HALF = jnp.float32, jnp.bfloat16
TABLE_SHAPE = (TABLE, Q, BS)
DIAG = (BS, BS)


def sems(count):
    return pltpu.SemaphoreType.DMA((count,))


def floats(*shape):
    return pltpu.VMEM(shape, FLOAT)


def call(kernel, takes, gives, outputs, scratch):
    shapes = [jax.ShapeDtypeStruct(o, t) for o, t in outputs]
    several = len(shapes) > 1
    specs = [SPACES[g] for g in gives]
    return pl.pallas_call(
        kernel,
        in_specs=[SPACES[t] for t in takes],
        out_specs=specs if several else specs[0],
        out_shape=shapes if several else shapes[0],
        scratch_shapes=scratch,
        compiler_params=pltpu.CompilerParams(vmem_limit_bytes=VMEM),
    )


send = call(
    send_kernel,
    "aa",
    "v",
    [((NP * SENT, BS), FLOAT)],
    [pltpu.SMEM((SLOTS, ROWS), jnp.int32), floats(*DIAG), sems(2)],
)
select = call(
    select_kernel,
    "asv",
    "v",
    [((NP, WANT, Q, BS), FLOAT)],
    [pltpu.SMEM((NP * TILES,), jnp.int32), sems(1)],
)
blocks = [floats(WANT * Q * PITCH, BS)]
xs_out = [((2, TILES, BS, BS), HALF), ((2, OWN, BS, BS), HALF)]
held_out = [((OWN, WIDE, BS, BS), FLOAT)]
half_out = [((OWN, SLOTS, BS, BS), FLOAT)] * 2
diag_out = [(DIAG, FLOAT)]
sums_out = [((NP * OWN * Q, BS), FLOAT)]
middle, final = (functools.partial(sweep_kernel, last) for last in (False, True))
first_call = call(first_kernel, "svvvv", "vvvv", xs_out + held_out + sums_out, blocks)
sweep_call = call(middle, "svvvvv", "vvv", held_out + diag_out + sums_out, blocks)
last_call = call(final, "svvvvv", "vvv", half_out + diag_out, blocks)


def to_mate(value):
    return lax.ppermute(value, "k", [(0, 1), (1, 0)])


def swapped(value):
    flat = value.reshape(NP, -1, BS)
    return lax.all_to_all(flat, PEERS, split_axis=0, concat_axis=0, tiled=True)


def on_device(omega_tiles, omega_diag, samples, pattern):
    core = lax.axis_index("k").astype(jnp.int32)
    at = jnp.stack([core, lax.axis_index("y").astype(jnp.int32)])
    in_pairs = omega_tiles.reshape(OWN, CORE, SLOTS, BS, BS)
    other = to_mate(jnp.where(core == 0, in_pairs[:, 1], in_pairs[:, 0]))
    plane = lax.axis_index("zh").astype(jnp.int32).reshape(1)
    came = swapped(send(pattern.T, samples))
    block = came[:, Q, :TILES].astype(jnp.int32)
    row, member = block // ROWS, block % ROWS
    place = (row % Z) // ZL * NP + (row // Z * ZL + row % ZL) * ROWS + turned(member)
    place = place.reshape(NP * TILES)

    def exchanged(mine):
        table = lax.all_gather(mine.reshape(NP * Q, BS), "zh").reshape(TABLE_SHAPE)
        return swapped(select(place, plane, table)).reshape(NP * WANT * Q, BS)

    got = exchanged(came[:, :Q])
    xj, xi, tiles, sums = first_call(at, got, omega_tiles, other, omega_diag)
    diag = omega_diag
    for sweep in range(ITERS):
        parts = swapped(sums).reshape(GROUPS, CORE, Y, OWN * Q, BS)
        got = exchanged(parts.sum(axis=2))
        if sweep < ITERS - 1:
            tiles, diag, sums = sweep_call(at, got, tiles, diag, xj, xi)
        else:
            kept, given, diag = last_call(at, got, tiles, diag, xj, xi)
    taken = to_mate(given)
    even = jnp.where(core == 0, kept, taken)
    odd = jnp.where(core == 0, taken, kept)
    return jnp.stack([even, odd], axis=1).reshape(omega_tiles.shape), diag


def solution(mesh):
    fine = Mesh(mesh.devices.reshape(X, ZH, ZL, Y, CORE), ("x", "zh", "zl", "y", "k"))
    rows = ("x", "zh", "zl")
    in_specs = (
        P(rows, COL, None, None),
        P(rows + COL, None),
        P(rows + COL, None),
        P(rows, COL),
    )
    out_specs = (P(rows, COL, None, None), P(rows + COL, None))
    return jax.shard_map(
        on_device, mesh=fine, in_specs=in_specs, out_specs=out_specs, check_vma=False
    )
```

time: 277 us -> 269 us (0.971)
  blocking collectives: 191 us -> 181 us
  starting transfers between devices: 21.7 us -> 27.4 us
  waiting for transfers between devices: 37.7 us -> 32.5 us
    all_to_all x4, blocking collectives: 111 us -> 99.6 us  [swapped(): return lax.all_to_all(flat, PEERS, split_axis=0, concat_axis=0, tiled=True)]
    all_to_all x2, waiting for transfers between devices: 37.7 us -> 28.8 us  [swapped(): return lax.all_to_all(flat, PEERS, split_axis=0, concat_axis=0, tiled=True)]
    ppermute x0 -> x2, starting transfers between devices: none -> 6.04 us  [to_mate(): return lax.ppermute(value, 'k', [(0, 1), (1, 0)])]
    ppermute x0 -> x2, waiting for transfers between devices: none -> 3.7 us  [to_mate(): return lax.ppermute(value, 'k', [(0, 1), (1, 0)])]
  transfers between devices with their start and end apart: 2 -> 4, of which waited for: 2 -> 4; matrix products, arithmetic and copies ran while one was open for 0% -> 0% of each run, Pallas kernels for 0% -> 0%
where the time goes in v3:
time: 269 us; the launch traced here: 268 us
  blocking collectives  181 us (67%)
  waiting for transfers between devices  32.5 us (12%)
  starting transfers between devices  27.4 us (10%)
  Pallas kernels  22.4 us (8%)
  local copies, waits for them, and re-layouts  2.89 us (1%)
    all_to_all x4, blocking collectives, swapped(): return lax.all_to_all(flat, PEERS, split_axis=0, concat_axis=0, tiled=True)  99.6 us
    all_gather x3, blocking collectives, exchanged(): table = lax.all_gather(mine.reshape(NP * Q, BS), 'zh').reshape(TABLE_SHAPE)  81.8 us
    all_to_all x2, waiting for transfers between devices, swapped(): return lax.all_to_all(flat, PEERS, split_axis=0, concat_axis=0, tiled=True)  28.8 us
    all_to_all x2, starting transfers between devices, swapped(): return lax.all_to_all(flat, PEERS, split_axis=0, concat_axis=0, tiled=True)  21.3 us
    pallas_call x3, Pallas kernels, exchanged(): return swapped(select(place, plane, table)).reshape(NP * WANT * Q, BS)  9.02 us
    ppermute x2, starting transfers between devices, to_mate(): return lax.ppermute(value, 'k', [(0, 1), (1, 0)])  6.04 us
  transfers between devices with their start and end apart: 4, of which 4 were waited for; matrix products, arithmetic and copies ran while one was open for 0% of the time, Pallas kernels for 0%

profile of v3, /device:TPU:1, one launch (start us, length us, event | category | flops | bytes accessed | tf_op | source)
XLA Modules:
  0.0 267.9 jit_solution(10360463742341027740)
XLA Ops:
  0.6 0.0 copy-start.2
  0.6 0.8 copy-done.2
  1.5 0.0 copy-start.3
  1.5 0.7 copy-done.3
  2.2 1.3 shard_map.59
  3.5 11.0 %all-to-all-start = ((f32[64,4,128]{2,1,0:T(4,128)}), f32[64,4,128]{2,1,0:T(4,128)S(1)}, u32[]{:S(2)}, u32[]{:S(2)}) async-start(f32[64,4,128]{2,1,0:T(4,128)} %bitcast.3), calls=%async_computation | async-start | bytes 262144 | tf_op jit(solution)/shard_map/all_to_all | solution.py:276
  14.4 8.3 %all-to-all-done = f32[64,4,128]{2,1,0:T(4,128)S(1)} async-done(((f32[64,4,128]{2,1,0:T(4,128)}), f32[64,4,128]{2,1,0:T(4,128)S(1)}, u32[]{:S(2)}, u32[]{:S(2)}) %all-to-all-start) | async-done | bytes 131104 | tf_op jit(solution)/shard_map/all_to_all | solution.py:276
  22.8 0.1 fusion.2
  22.9 0.1 convert_element_type.8
  23.1 31.5 %all_gather.9 = f32[8,128,128]{2,1,0:T(8,128)S(1)} all-gather(f32[1,128,128]{2,1,0:T(8,128)S(1)} %bitcast.55), channel_id=1, replica_groups=mesh['x'=4,'zh'=8,'zl'=2,'y'=4,'k'=2] {'zh'}, dimensions={0}, use_global_device_ids=true | all-gather | bytes 589824 | tf_op jit(solution)/shard_map/all_gather | solution.py:292
  54.5 3.8 %shard_map.60 = f32[64,28,2,128]{3,2,1,0:T(2,128)} custom-call(s32[1536]{0:T(1024)S(1)} %fusion.6.place, s32[1]{0:T(128)} %bitcast.4.plane, f32[512,2,128]{2,1,0:T(2,128)S(1)} %bitcast.45), custom_call_target="tpu_custom_call" | custom-call | tf_op jit(solution)/shard_map/pallas_call | solution.py:293
  58.4 0.0 copy-start
  58.4 10.3 %all-to-all-start.1 = ((f32[64,56,128]{2,1,0:T(8,128)}), f32[64,56,128]{2,1,0:T(8,128)}, u32[]{:S(2)}, u32[]{:S(2)}) async-start(f32[64,56,128]{2,1,0:T(8,128)} %bitcast.7), calls=%async_computation.1 | async-start | bytes 3670016 | tf_op jit(solution)/shard_map/all_to_all | solution.py:276
  68.7 0.0 copy-start.1
  68.8 0.0 copy-done
  68.8 0.1 fusion.1
  68.9 2.5 collective-permute-start
  71.4 0.1 pad_add_fusion.at
  71.5 1.8 collective-permute-done.other
  73.3 20.4 %all-to-all-done.1 = f32[64,56,128]{2,1,0:T(8,128)} async-done(((f32[64,56,128]{2,1,0:T(8,128)}), f32[64,56,128]{2,1,0:T(8,128)}, u32[]{:S(2)}, u32[]{:S(2)}) %all-to-all-start.1) | async-done | bytes 1835040 | tf_op jit(solution)/shard_map/all_to_all | solution.py:276
  93.7 0.0 copy-done.1
  93.7 3.3 %shard_map.61 = (bf16[2,24,128,128]{3,2,1,0:T(8,128)(2,1)S(1)}, bf16[2,4,128,128]{3,2,1,0:T(8,128)(2,1)S(1)}, f32[4,6,128,128]{3,2,1,0:T(8,128)S(1)}, f32[512,128]{1,0:T(8,128)S(1)}) custom-call(s32[2]{0:T(128)S(1)} %pad_add_fusion.at, f32[3584,128]{1,0:T(8,128)} %bitcast.8.recv, f32[8,3,128,128]{3,2,1,0:T(8,128)S(1)} %copy-done, ...), custom_call_target="tpu_custom_call" | custom-call | tf_op jit(solution)/shard_map/pallas_call | solution.py:296
  97.0 15.0 %all_to_all.30 = f32[64,8,128]{2,1,0:T(8,128)S(1)} all-to-all(f32[64,8,128]{2,1,0:T(8,128)S(1)} %bitcast.47), channel_id=1, replica_groups=mesh['x'=4,'zh'=8,'zl'=2,'y'=4,'k'=2] {'x','zl','k','y'}, dimensions={0} | all-to-all | bytes 524288 | tf_op jit(solution)/shard_map/all_to_all | solution.py:276
  112.0 25.2 %all_gather.10 = f32[8,128,128]{2,1,0:T(8,128)S(1)} all-gather(f32[1,128,128]{2,1,0:T(8,128)S(1)} %bitcast.53), channel_id=1, replica_groups=mesh['x'=4,'zh'=8,'zl'=2,'y'=4,'k'=2] {'zh'}, dimensions={0}, use_global_device_ids=true | all-gather | bytes 589824 | tf_op jit(solution)/shard_map/all_gather | solution.py:292
  137.1 2.6 shard_map.62
  139.7 34.8 %all_to_all.31 = f32[64,56,128]{2,1,0:T(8,128)} all-to-all(f32[64,56,128]{2,1,0:T(8,128)S(1)} %bitcast.42), channel_id=1, replica_groups=mesh['x'=4,'zh'=8,'zl'=2,'y'=4,'k'=2] {'x','zl','k','y'}, dimensions={0} | all-to-all | bytes 3670016 | tf_op jit(solution)/shard_map/all_to_all | solution.py:276
  174.5 4.6 %shard_map.63 = (f32[4,6,128,128]{3,2,1,0:T(8,128)S(1)}, f32[128,128]{1,0:T(8,128)S(1)}, f32[512,128]{1,0:T(8,128)S(1)}) custom-call(s32[2]{0:T(128)S(1)} %pad_add_fusion.at, f32[3584,128]{1,0:T(8,128)} %bitcast.51, f32[4,6,128,128]{3,2,1,0:T(8,128)S(1)} %get-tuple-element.13.tiles, f32[128,128]{1,0:T(8,128)S(1)} %copy-done.1, ...), custom_call_target="tpu_custom_call" | custom-call | tf_op jit(solution)/shard_map/pallas_call | solution.py:302
  179.2 15.0 %all_to_all.32 = f32[64,8,128]{2,1,0:T(8,128)S(1)} all-to-all(f32[64,8,128]{2,1,0:T(8,128)S(1)} %bitcast.48), channel_id=1, replica_groups=mesh['x'=4,'zh'=8,'zl'=2,'y'=4,'k'=2] {'x','zl','k','y'}, dimensions={0} | all-to-all | bytes 524288 | tf_op jit(solution)/shard_map/all_to_all | solution.py:276
  194.2 25.2 %all_gather.11 = f32[8,128,128]{2,1,0:T(8,128)S(1)} all-gather(f32[1,128,128]{2,1,0:T(8,128)S(1)} %bitcast.54), channel_id=1, replica_groups=mesh['x'=4,'zh'=8,'zl'=2,'y'=4,'k'=2] {'zh'}, dimensions={0}, use_global_device_ids=true | all-gather | bytes 589824 | tf_op jit(solution)/shard_map/all_gather | solution.py:292
  219.3 2.6 shard_map.64
  221.9 34.9 %all_to_all.33 = f32[64,56,128]{2,1,0:T(8,128)} all-to-all(f32[64,56,128]{2,1,0:T(8,128)S(1)} %bitcast.41), channel_id=1, replica_groups=mesh['x'=4,'zh'=8,'zl'=2,'y'=4,'k'=2] {'x','zl','k','y'}, dimensions={0} | all-to-all | bytes 3670016 | tf_op jit(solution)/shard_map/all_to_all | solution.py:276
  256.8 4.2 %shard_map.65 = (f32[4,3,128,128]{3,2,1,0:T(8,128)S(1)}, f32[4,3,128,128]{3,2,1,0:T(8,128)S(1)}, f32[128,128]{1,0:T(8,128)}) custom-call(s32[2]{0:T(128)S(1)} %pad_add_fusion.at, f32[3584,128]{1,0:T(8,128)} %bitcast.50, f32[4,6,128,128]{3,2,1,0:T(8,128)S(1)} %get-tuple-element.17.tiles, f32[128,128]{1,0:T(8,128)S(1)} %get-tuple-element.18.diag, ...), custom_call_target="tpu_custom_call" | custom-call | tf_op jit(solution)/shard_map/pallas_call | solution.py:304
  261.0 3.5 %collective-permute-start.1 = (f32[4,3,128,128]{3,2,1,0:T(8,128)S(1)}, f32[4,3,128,128]{3,2,1,0:T(8,128)S(1)}, u32[]{:S(2)}, u32[]{:S(2)}) collective-permute-start(f32[4,3,128,128]{3,2,1,0:T(8,128)S(1)} %get-tuple-element.20), channel_id=1, source_target_pairs={{0,1},{1,0},{2,3},{3,2},{4,5},{5,4},{6,7},{7,6},{8,9},{9,8},{10,11... | collective-permute-start | bytes 2359304 | tf_op jit(solution)/shard_map/ppermute | solution.py:271
  264.5 1.9 collective-permute-done.1
  266.4 0.1 select_bitcast_fusion.1
  266.5 0.1 pad_maximum_fusion
  266.7 1.3 copy.15
  (4 shorter events, 0.1 us)
Async XLA Ops:
  0.6 0.8 copy-start.2
  1.5 0.7 copy-start.3
  3.5 19.3 %all-to-all-start = ((f32[64,4,128]{2,1,0:T(4,128)}), f32[64,4,128]{2,1,0:T(4,128)S(1)}, u32[]{:S(2)}, u32[]{:S(2)}) async-start(f32[64,4,128]{2,1,0:T(4,128)} %bitcast.3), calls=%async_computation | async-start | bytes 262144 | tf_op jit(solution)/shard_map/all_to_all | solution.py:276
  58.4 10.4 %copy-start = (f32[8,3,128,128]{3,2,1,0:T(8,128)S(1)}, f32[8,3,128,128]{3,2,1,0:T(8,128)}, u32[]{:S(2)}) copy-start(f32[8,3,128,128]{3,2,1,0:T(8,128)} %tiles.1) | copy-start | bytes 4718596
  58.4 35.3 %all-to-all-start.1 = ((f32[64,56,128]{2,1,0:T(8,128)}), f32[64,56,128]{2,1,0:T(8,128)}, u32[]{:S(2)}, u32[]{:S(2)}) async-start(f32[64,56,128]{2,1,0:T(8,128)} %bitcast.7), calls=%async_computation.1 | async-start | bytes 3670016 | tf_op jit(solution)/shard_map/all_to_all | solution.py:276
  68.7 25.0 %copy-start.1 = (f32[128,128]{1,0:T(8,128)S(1)}, f32[128,128]{1,0:T(8,128)}, u32[]{:S(2)}) copy-start(f32[128,128]{1,0:T(8,128)} %diag.3) | copy-start | bytes 196612
  68.9 4.4 %collective-permute-start = (f32[4,3,128,128]{3,2,1,0:T(8,128)S(1)}, f32[4,3,128,128]{3,2,1,0:T(8,128)S(1)}, u32[]{:S(2)}, u32[]{:S(2)}) collective-permute-start(f32[4,3,128,128]{3,2,1,0:T(8,128)S(1)} %fusion.1), channel_id=1, source_target_pairs={{0,1},{1,0},{2,3},{3,2},{4,5},{5,4},{6,7},{7,6},{8,9},{9,8},{10,11... | collective-permute-start | bytes 2359304 | tf_op jit(solution)/shard_map/ppermute | solution.py:271
  261.0 5.4 %collective-permute-start.1 = (f32[4,3,128,128]{3,2,1,0:T(8,128)S(1)}, f32[4,3,128,128]{3,2,1,0:T(8,128)S(1)}, u32[]{:S(2)}, u32[]{:S(2)}) collective-permute-start(f32[4,3,128,128]{3,2,1,0:T(8,128)S(1)} %get-tuple-element.20), channel_id=1, source_target_pairs={{0,1},{1,0},{2,3},{3,2},{4,5},{5,4},{6,7},{7,6},{8,9},{9,8},{10,11... | collective-permute-start | bytes 2359304 | tf_op jit(solution)/shard_map/ppermute | solution.py:271

commit v4 on v3

--- a/solution.py
+++ b/solution.py
@@ -209,6 +209,12 @@
 
 
 FIRST_UNROLL = 2
+def merge_kernel(at, kept, taken, out, sems):
+    mine, other = out.at[:, at[0]], out.at[:, 1 - at[0]]
+    for copy in loading([kept, taken], [mine, other], sems):
+        copy.wait()
+
+
 SPACES = {
     "s": pl.BlockSpec(memory_space=pltpu.SMEM),
     "v": pl.BlockSpec(memory_space=pltpu.VMEM),
@@ -267,6 +273,9 @@
 last_call = call(final, "svvvvv", "vvv", half_out + diag_out, blocks)
 
 
+merge = call(merge_kernel, "saa", "a", [((OWN, CORE, SLOTS, BS, BS), FLOAT)], [sems(2)])
+
+
 def to_mate(value):
     return lax.ppermute(value, "k", [(0, 1), (1, 0)])
 
@@ -303,9 +312,7 @@
         else:
             kept, given, diag = last_call(at, got, tiles, diag, xj, xi)
     taken = to_mate(given)
-    even = jnp.where(core == 0, kept, taken)
-    odd = jnp.where(core == 0, taken, kept)
-    return jnp.stack([even, odd], axis=1).reshape(omega_tiles.shape), diag
+    return merge(at, kept, taken).reshape(omega_tiles.shape), diag
 
 
 def solution(mesh):

time: 269 us -> 269 us (level)
  no operation moved by 1% of the time
where the time goes in v4:
time: 269 us; the launch traced here: 268 us
  blocking collectives  181 us (67%)
  waiting for transfers between devices  32.5 us (12%)
  starting transfers between devices  27.4 us (10%)
  Pallas kernels  24.1 us (9%)
    all_to_all x4, blocking collectives, swapped(): return lax.all_to_all(flat, PEERS, split_axis=0, concat_axis=0, tiled=True)  99.3 us
    all_gather x3, blocking collectives, exchanged(): table = lax.all_gather(mine.reshape(NP * Q, BS), 'zh').reshape(TABLE_SHAPE)  82.2 us
    all_to_all x2, waiting for transfers between devices, swapped(): return lax.all_to_all(flat, PEERS, split_axis=0, concat_axis=0, tiled=True)  28.8 us
    all_to_all x2, starting transfers between devices, swapped(): return lax.all_to_all(flat, PEERS, split_axis=0, concat_axis=0, tiled=True)  21.3 us
    pallas_call x3, Pallas kernels, exchanged(): return swapped(select(place, plane, table)).reshape(NP * WANT * Q, BS)  9.01 us
    ppermute x2, starting transfers between devices, to_mate(): return lax.ppermute(value, 'k', [(0, 1), (1, 0)])  6.05 us
  transfers between devices with their start and end apart: 4, of which 4 were waited for; matrix products, arithmetic and copies ran while one was open for 0% of the time, Pallas kernels for 0%

profile of v4, /device:TPU:1, one launch (start us, length us, event | category | flops | bytes accessed | tf_op | source)
XLA Modules:
  0.0 268.1 jit_solution(6641678537154101541)
XLA Ops:
  0.6 0.0 copy-start.2
  0.6 0.8 copy-done.2
  1.5 0.0 copy-start.3
  1.5 0.7 copy-done.3
  2.2 1.3 shard_map.59
  3.5 11.0 %all-to-all-start = ((f32[64,4,128]{2,1,0:T(4,128)}), f32[64,4,128]{2,1,0:T(4,128)S(1)}, u32[]{:S(2)}, u32[]{:S(2)}) async-start(f32[64,4,128]{2,1,0:T(4,128)} %bitcast.3), calls=%async_computation | async-start | bytes 262144 | tf_op jit(solution)/shard_map/all_to_all | solution.py:285
  14.4 8.3 %all-to-all-done = f32[64,4,128]{2,1,0:T(4,128)S(1)} async-done(((f32[64,4,128]{2,1,0:T(4,128)}), f32[64,4,128]{2,1,0:T(4,128)S(1)}, u32[]{:S(2)}, u32[]{:S(2)}) %all-to-all-start) | async-done | bytes 131104 | tf_op jit(solution)/shard_map/all_to_all | solution.py:285
  22.8 0.1 fusion.2
  22.9 0.1 convert_element_type.8
  23.1 31.5 %all_gather.9 = f32[8,128,128]{2,1,0:T(8,128)S(1)} all-gather(f32[1,128,128]{2,1,0:T(8,128)S(1)} %bitcast.51), channel_id=1, replica_groups=mesh['x'=4,'zh'=8,'zl'=2,'y'=4,'k'=2] {'zh'}, dimensions={0}, use_global_device_ids=true | all-gather | bytes 589824 | tf_op jit(solution)/shard_map/all_gather | solution.py:301
  54.5 3.8 %shard_map.60 = f32[64,28,2,128]{3,2,1,0:T(2,128)} custom-call(s32[1536]{0:T(1024)S(1)} %fusion.6.place, s32[1]{0:T(128)} %bitcast.4.plane, f32[512,2,128]{2,1,0:T(2,128)S(1)} %bitcast.41), custom_call_target="tpu_custom_call" | custom-call | tf_op jit(solution)/shard_map/pallas_call | solution.py:302
  58.4 0.0 copy-start
  58.4 10.3 %all-to-all-start.1 = ((f32[64,56,128]{2,1,0:T(8,128)}), f32[64,56,128]{2,1,0:T(8,128)}, u32[]{:S(2)}, u32[]{:S(2)}) async-start(f32[64,56,128]{2,1,0:T(8,128)} %bitcast.7), calls=%async_computation.1 | async-start | bytes 3670016 | tf_op jit(solution)/shard_map/all_to_all | solution.py:285
  68.7 0.0 copy-start.1
  68.7 0.0 copy-done
  68.8 0.1 fusion.1
  68.8 2.5 collective-permute-start
  71.4 0.1 pad_add_fusion.at
  71.5 1.8 collective-permute-done.other
  73.3 20.4 %all-to-all-done.1 = f32[64,56,128]{2,1,0:T(8,128)} async-done(((f32[64,56,128]{2,1,0:T(8,128)}), f32[64,56,128]{2,1,0:T(8,128)}, u32[]{:S(2)}, u32[]{:S(2)}) %all-to-all-start.1) | async-done | bytes 1835040 | tf_op jit(solution)/shard_map/all_to_all | solution.py:285
  93.7 0.0 copy-done.1
  93.7 3.3 %shard_map.61 = (bf16[2,24,128,128]{3,2,1,0:T(8,128)(2,1)S(1)}, bf16[2,4,128,128]{3,2,1,0:T(8,128)(2,1)S(1)}, f32[4,6,128,128]{3,2,1,0:T(8,128)S(1)}, f32[512,128]{1,0:T(8,128)S(1)}) custom-call(s32[2]{0:T(128)S(1)} %pad_add_fusion.at, f32[3584,128]{1,0:T(8,128)} %bitcast.8.recv, f32[8,3,128,128]{3,2,1,0:T(8,128)S(1)} %copy-done, ...), custom_call_target="tpu_custom_call" | custom-call | tf_op jit(solution)/shard_map/pallas_call | solution.py:305
  97.0 15.0 %all_to_all.30 = f32[64,8,128]{2,1,0:T(8,128)S(1)} all-to-all(f32[64,8,128]{2,1,0:T(8,128)S(1)} %bitcast.43), channel_id=1, replica_groups=mesh['x'=4,'zh'=8,'zl'=2,'y'=4,'k'=2] {'x','zl','k','y'}, dimensions={0} | all-to-all | bytes 524288 | tf_op jit(solution)/shard_map/all_to_all | solution.py:285
  112.0 25.1 %all_gather.10 = f32[8,128,128]{2,1,0:T(8,128)S(1)} all-gather(f32[1,128,128]{2,1,0:T(8,128)S(1)} %bitcast.49), channel_id=1, replica_groups=mesh['x'=4,'zh'=8,'zl'=2,'y'=4,'k'=2] {'zh'}, dimensions={0}, use_global_device_ids=true | all-gather | bytes 589824 | tf_op jit(solution)/shard_map/all_gather | solution.py:301
  137.1 2.6 shard_map.62
  139.7 34.8 %all_to_all.31 = f32[64,56,128]{2,1,0:T(8,128)} all-to-all(f32[64,56,128]{2,1,0:T(8,128)S(1)} %bitcast.38), channel_id=1, replica_groups=mesh['x'=4,'zh'=8,'zl'=2,'y'=4,'k'=2] {'x','zl','k','y'}, dimensions={0} | all-to-all | bytes 3670016 | tf_op jit(solution)/shard_map/all_to_all | solution.py:285
  174.5 4.6 %shard_map.63 = (f32[4,6,128,128]{3,2,1,0:T(8,128)S(1)}, f32[128,128]{1,0:T(8,128)S(1)}, f32[512,128]{1,0:T(8,128)S(1)}) custom-call(s32[2]{0:T(128)S(1)} %pad_add_fusion.at, f32[3584,128]{1,0:T(8,128)} %bitcast.47, f32[4,6,128,128]{3,2,1,0:T(8,128)S(1)} %get-tuple-element.13.tiles, f32[128,128]{1,0:T(8,128)S(1)} %copy-done.1, ...), custom_call_target="tpu_custom_call" | custom-call | tf_op jit(solution)/shard_map/pallas_call | solution.py:311
  179.1 14.9 %all_to_all.32 = f32[64,8,128]{2,1,0:T(8,128)S(1)} all-to-all(f32[64,8,128]{2,1,0:T(8,128)S(1)} %bitcast.44), channel_id=1, replica_groups=mesh['x'=4,'zh'=8,'zl'=2,'y'=4,'k'=2] {'x','zl','k','y'}, dimensions={0} | all-to-all | bytes 524288 | tf_op jit(solution)/shard_map/all_to_all | solution.py:285
  194.1 25.6 %all_gather.11 = f32[8,128,128]{2,1,0:T(8,128)S(1)} all-gather(f32[1,128,128]{2,1,0:T(8,128)S(1)} %bitcast.50), channel_id=1, replica_groups=mesh['x'=4,'zh'=8,'zl'=2,'y'=4,'k'=2] {'zh'}, dimensions={0}, use_global_device_ids=true | all-gather | bytes 589824 | tf_op jit(solution)/shard_map/all_gather | solution.py:301
  219.6 2.6 shard_map.64
  222.2 34.6 %all_to_all.33 = f32[64,56,128]{2,1,0:T(8,128)} all-to-all(f32[64,56,128]{2,1,0:T(8,128)S(1)} %bitcast.37), channel_id=1, replica_groups=mesh['x'=4,'zh'=8,'zl'=2,'y'=4,'k'=2] {'x','zl','k','y'}, dimensions={0} | all-to-all | bytes 3670016 | tf_op jit(solution)/shard_map/all_to_all | solution.py:285
  256.8 4.2 %shard_map.65 = (f32[4,3,128,128]{3,2,1,0:T(8,128)S(1)}, f32[4,3,128,128]{3,2,1,0:T(8,128)S(1)}, f32[128,128]{1,0:T(8,128)}) custom-call(s32[2]{0:T(128)S(1)} %pad_add_fusion.at, f32[3584,128]{1,0:T(8,128)} %bitcast.46, f32[4,6,128,128]{3,2,1,0:T(8,128)S(1)} %get-tuple-element.17.tiles, f32[128,128]{1,0:T(8,128)S(1)} %get-tuple-element.18.diag, ...), custom_call_target="tpu_custom_call" | custom-call | tf_op jit(solution)/shard_map/pallas_call | solution.py:313
  261.0 3.5 %collective-permute-start.1 = (f32[4,3,128,128]{3,2,1,0:T(8,128)S(1)}, f32[4,3,128,128]{3,2,1,0:T(8,128)S(1)}, u32[]{:S(2)}, u32[]{:S(2)}) collective-permute-start(f32[4,3,128,128]{3,2,1,0:T(8,128)S(1)} %get-tuple-element.20), channel_id=1, source_target_pairs={{0,1},{1,0},{2,3},{3,2},{4,5},{5,4},{6,7},{7,6},{8,9},{9,8},{10,11... | collective-permute-start | bytes 2359304 | tf_op jit(solution)/shard_map/ppermute | solution.py:280
  264.5 1.9 collective-permute-done.1.taken
  266.4 1.7 shard_map.66
  (4 shorter events, 0.1 us)
Async XLA Ops:
  0.6 0.8 copy-start.2
  1.5 0.7 copy-start.3
  3.5 19.3 %all-to-all-start = ((f32[64,4,128]{2,1,0:T(4,128)}), f32[64,4,128]{2,1,0:T(4,128)S(1)}, u32[]{:S(2)}, u32[]{:S(2)}) async-start(f32[64,4,128]{2,1,0:T(4,128)} %bitcast.3), calls=%async_computation | async-start | bytes 262144 | tf_op jit(solution)/shard_map/all_to_all | solution.py:285
  58.4 10.4 %copy-start = (f32[8,3,128,128]{3,2,1,0:T(8,128)S(1)}, f32[8,3,128,128]{3,2,1,0:T(8,128)}, u32[]{:S(2)}) copy-start(f32[8,3,128,128]{3,2,1,0:T(8,128)} %tiles.1) | copy-start | bytes 4718596
  58.4 35.3 %all-to-all-start.1 = ((f32[64,56,128]{2,1,0:T(8,128)}), f32[64,56,128]{2,1,0:T(8,128)}, u32[]{:S(2)}, u32[]{:S(2)}) async-start(f32[64,56,128]{2,1,0:T(8,128)} %bitcast.7), calls=%async_computation.1 | async-start | bytes 3670016 | tf_op jit(solution)/shard_map/all_to_all | solution.py:285
  68.7 25.0 %copy-start.1 = (f32[128,128]{1,0:T(8,128)S(1)}, f32[128,128]{1,0:T(8,128)}, u32[]{:S(2)}) copy-start(f32[128,128]{1,0:T(8,128)} %diag.3) | copy-start | bytes 196612
  68.8 4.4 %collective-permute-start = (f32[4,3,128,128]{3,2,1,0:T(8,128)S(1)}, f32[4,3,128,128]{3,2,1,0:T(8,128)S(1)}, u32[]{:S(2)}, u32[]{:S(2)}) collective-permute-start(f32[4,3,128,128]{3,2,1,0:T(8,128)S(1)} %fusion.1), channel_id=1, source_target_pairs={{0,1},{1,0},{2,3},{3,2},{4,5},{5,4},{6,7},{7,6},{8,9},{9,8},{10,11... | collective-permute-start | bytes 2359304 | tf_op jit(solution)/shard_map/ppermute | solution.py:280
  261.0 5.4 %collective-permute-start.1 = (f32[4,3,128,128]{3,2,1,0:T(8,128)S(1)}, f32[4,3,128,128]{3,2,1,0:T(8,128)S(1)}, u32[]{:S(2)}, u32[]{:S(2)}) collective-permute-start(f32[4,3,128,128]{3,2,1,0:T(8,128)S(1)} %get-tuple-element.20), channel_id=1, source_target_pairs={{0,1},{1,0},{2,3},{3,2},{4,5},{5,4},{6,7},{7,6},{8,9},{9,8},{10,11... | collective-permute-start | bytes 2359304 | tf_op jit(solution)/shard_map/ppermute | solution.py:280

commit v5 on v3

--- a/solution.py
+++ b/solution.py
@@ -73,7 +73,9 @@
         out[pl.ds(q, NP, stride=SENT), :] = listed
 
 
-def select_kernel(place, plane, table, out, numbers, sems):
+def select_kernel(chunks, place, plane, table, target, *rest):
+    *out, numbers, sems = rest
+    out = out[0] if chunks else target
     [copy] = loading([place], [numbers], sems)
 
     def rows(d, carry):
@@ -94,7 +96,18 @@
                 out[pair[core], t] = table[numbers[base + entry]]
         return carry
 
-    lax.fori_loop(0, NP // CORE, columns, 0)
+    if not chunks:
+        lax.fori_loop(0, NP // CORE, columns, 0)
+        return
+    stores = []
+    for n in range(chunks):
+        count = NP // CORE // chunks
+        lax.fori_loop(n * count, (n + 1) * count, columns, 0)
+        peers = pl.ds(n * count * CORE, count * CORE)
+        stores.append(pltpu.make_async_copy(out.at[peers], target.at[peers], sems.at[1 + n]))
+        stores[n].start()
+    for store in stores:
+        store.wait()
 
 
 def loading(sources, places, sems):
@@ -248,13 +261,13 @@
     [((NP * SENT, BS), FLOAT)],
     [pltpu.SMEM((SLOTS, ROWS), jnp.int32), floats(*DIAG), sems(2)],
 )
-select = call(
-    select_kernel,
-    "asv",
-    "v",
-    [((NP, WANT, Q, BS), FLOAT)],
-    [pltpu.SMEM((NP * TILES,), jnp.int32), sems(1)],
-)
+CHUNKS = 4
+SELECTED = (NP, WANT, Q, BS)
+numbers = [pltpu.SMEM((NP * TILES,), jnp.int32), sems(1 + CHUNKS)]
+to_vmem = functools.partial(select_kernel, 0)
+to_hbm = functools.partial(select_kernel, CHUNKS)
+select = call(to_vmem, "asv", "v", [(SELECTED, FLOAT)], numbers)
+select_first = call(to_hbm, "asv", "a", [(SELECTED, FLOAT)], [floats(*SELECTED)] + numbers)
 blocks = [floats(WANT * Q * PITCH, BS)]
 xs_out = [((2, TILES, BS, BS), HALF), ((2, OWN, BS, BS), HALF)]
 held_out = [((OWN, WIDE, BS, BS), FLOAT)]
@@ -288,16 +301,16 @@
     place = (row % Z) // ZL * NP + (row // Z * ZL + row % ZL) * ROWS + turned(member)
     place = place.reshape(NP * TILES)
 
-    def exchanged(mine):
+    def exchanged(mine, select):
         table = lax.all_gather(mine.reshape(NP * Q, BS), "zh").reshape(TABLE_SHAPE)
         return swapped(select(place, plane, table)).reshape(NP * WANT * Q, BS)
 
-    got = exchanged(came[:, :Q])
+    got = exchanged(came[:, :Q], select_first)
     xj, xi, tiles, sums = first_call(at, got, omega_tiles, other, omega_diag)
     diag = omega_diag
     for sweep in range(ITERS):
         parts = swapped(sums).reshape(GROUPS, CORE, Y, OWN * Q, BS)
-        got = exchanged(parts.sum(axis=2))
+        got = exchanged(parts.sum(axis=2), select)
         if sweep < ITERS - 1:
             tiles, diag, sums = sweep_call(at, got, tiles, diag, xj, xi)
         else:

time: 269 us -> 268 us (level)
  no operation moved by 1% of the time
where the time goes in v5:
time: 268 us
  blocking collectives  181 us (68%)
  waiting for transfers between devices  32.5 us (12%)
  starting transfers between devices  27.4 us (10%)
  Pallas kernels  22 us (8%)
  local copies, waits for them, and re-layouts  2.89 us (1%)
    all_to_all x4, blocking collectives, swapped(): return lax.all_to_all(flat, PEERS, split_axis=0, concat_axis=0, tiled=True)  99.9 us
    all_gather x3, blocking collectives, exchanged(): table = lax.all_gather(mine.reshape(NP * Q, BS), 'zh').reshape(TABLE_SHAPE)  81.5 us
    all_to_all x2, waiting for transfers between devices, swapped(): return lax.all_to_all(flat, PEERS, split_axis=0, concat_axis=0, tiled=True)  28.8 us
    all_to_all x2, starting transfers between devices, swapped(): return lax.all_to_all(flat, PEERS, split_axis=0, concat_axis=0, tiled=True)  21.3 us
    pallas_call x3, Pallas kernels, exchanged(): return swapped(select(place, plane, table)).reshape(NP * WANT * Q, BS)  8.67 us
    ppermute x2, starting transfers between devices, to_mate(): return lax.ppermute(value, 'k', [(0, 1), (1, 0)])  6.05 us
  transfers between devices with their start and end apart: 4, of which 4 were waited for; matrix products, arithmetic and copies ran while one was open for 0% of the time, Pallas kernels for 0%

profile of v5, /device:TPU:1, one launch (start us, length us, event | category | flops | bytes accessed | tf_op | source)
XLA Modules:
  0.0 267.6 jit_solution(15315467073529233209)
XLA Ops:
  0.6 0.0 copy-start.2
  0.6 0.8 copy-done.2
  1.5 0.0 copy-start.3
  1.5 0.7 copy-done.3
  2.2 1.3 shard_map.59
  3.5 11.0 %all-to-all-start = ((f32[64,4,128]{2,1,0:T(4,128)}), f32[64,4,128]{2,1,0:T(4,128)S(1)}, u32[]{:S(2)}, u32[]{:S(2)}) async-start(f32[64,4,128]{2,1,0:T(4,128)} %bitcast.3), calls=%async_computation | async-start | bytes 262144 | tf_op jit(solution)/shard_map/all_to_all | solution.py:289
  14.4 8.3 %all-to-all-done = f32[64,4,128]{2,1,0:T(4,128)S(1)} async-done(((f32[64,4,128]{2,1,0:T(4,128)}), f32[64,4,128]{2,1,0:T(4,128)S(1)}, u32[]{:S(2)}, u32[]{:S(2)}) %all-to-all-start) | async-done | bytes 131104 | tf_op jit(solution)/shard_map/all_to_all | solution.py:289
  22.8 0.1 fusion.2
  22.9 0.1 convert_element_type.8
  23.1 31.5 %all_gather.9 = f32[8,128,128]{2,1,0:T(8,128)S(1)} all-gather(f32[1,128,128]{2,1,0:T(8,128)S(1)} %bitcast.55), channel_id=1, replica_groups=mesh['x'=4,'zh'=8,'zl'=2,'y'=4,'k'=2] {'zh'}, dimensions={0}, use_global_device_ids=true | all-gather | bytes 589824 | tf_op jit(solution)/shard_map/all_gather | solution.py:305
  54.5 3.4 %shard_map.60 = f32[64,28,2,128]{3,2,1,0:T(2,128)} custom-call(s32[1536]{0:T(1024)S(1)} %fusion.6.place, s32[1]{0:T(128)} %bitcast.4.plane, f32[512,2,128]{2,1,0:T(2,128)S(1)} %bitcast.45), custom_call_target="tpu_custom_call" | custom-call | tf_op jit(solution)/shard_map/pallas_call | solution.py:306
  57.9 0.0 copy-start
  58.0 10.3 %all-to-all-start.1 = ((f32[64,56,128]{2,1,0:T(8,128)}), f32[64,56,128]{2,1,0:T(8,128)}, u32[]{:S(2)}, u32[]{:S(2)}) async-start(f32[64,56,128]{2,1,0:T(8,128)} %bitcast.7), calls=%async_computation.1 | async-start | bytes 3670016 | tf_op jit(solution)/shard_map/all_to_all | solution.py:289
  68.3 0.0 copy-start.1
  68.3 0.0 copy-done
  68.3 0.1 fusion.1
  68.4 2.5 collective-permute-start
  71.0 0.1 pad_add_fusion.at
  71.0 1.8 collective-permute-done.other
  72.9 20.4 %all-to-all-done.1 = f32[64,56,128]{2,1,0:T(8,128)} async-done(((f32[64,56,128]{2,1,0:T(8,128)}), f32[64,56,128]{2,1,0:T(8,128)}, u32[]{:S(2)}, u32[]{:S(2)}) %all-to-all-start.1) | async-done | bytes 1835040 | tf_op jit(solution)/shard_map/all_to_all | solution.py:289
  93.3 0.0 copy-done.1
  93.3 3.3 %shard_map.61 = (bf16[2,24,128,128]{3,2,1,0:T(8,128)(2,1)S(1)}, bf16[2,4,128,128]{3,2,1,0:T(8,128)(2,1)S(1)}, f32[4,6,128,128]{3,2,1,0:T(8,128)S(1)}, f32[512,128]{1,0:T(8,128)S(1)}) custom-call(s32[2]{0:T(128)S(1)} %pad_add_fusion.at, f32[3584,128]{1,0:T(8,128)} %bitcast.8.recv, f32[8,3,128,128]{3,2,1,0:T(8,128)S(1)} %copy-done, ...), custom_call_target="tpu_custom_call" | custom-call | tf_op jit(solution)/shard_map/pallas_call | solution.py:309
  96.5 15.0 %all_to_all.30 = f32[64,8,128]{2,1,0:T(8,128)S(1)} all-to-all(f32[64,8,128]{2,1,0:T(8,128)S(1)} %bitcast.47), channel_id=1, replica_groups=mesh['x'=4,'zh'=8,'zl'=2,'y'=4,'k'=2] {'x','zl','k','y'}, dimensions={0} | all-to-all | bytes 524288 | tf_op jit(solution)/shard_map/all_to_all | solution.py:289
  111.6 25.1 %all_gather.10 = f32[8,128,128]{2,1,0:T(8,128)S(1)} all-gather(f32[1,128,128]{2,1,0:T(8,128)S(1)} %bitcast.53), channel_id=1, replica_groups=mesh['x'=4,'zh'=8,'zl'=2,'y'=4,'k'=2] {'zh'}, dimensions={0}, use_global_device_ids=true | all-gather | bytes 589824 | tf_op jit(solution)/shard_map/all_gather | solution.py:305
  136.7 2.6 shard_map.62
  139.3 34.8 %all_to_all.31 = f32[64,56,128]{2,1,0:T(8,128)} all-to-all(f32[64,56,128]{2,1,0:T(8,128)S(1)} %bitcast.42), channel_id=1, replica_groups=mesh['x'=4,'zh'=8,'zl'=2,'y'=4,'k'=2] {'x','zl','k','y'}, dimensions={0} | all-to-all | bytes 3670016 | tf_op jit(solution)/shard_map/all_to_all | solution.py:289
  174.1 4.6 %shard_map.63 = (f32[4,6,128,128]{3,2,1,0:T(8,128)S(1)}, f32[128,128]{1,0:T(8,128)S(1)}, f32[512,128]{1,0:T(8,128)S(1)}) custom-call(s32[2]{0:T(128)S(1)} %pad_add_fusion.at, f32[3584,128]{1,0:T(8,128)} %bitcast.51, f32[4,6,128,128]{3,2,1,0:T(8,128)S(1)} %get-tuple-element.13.tiles, f32[128,128]{1,0:T(8,128)S(1)} %copy-done.1, ...), custom_call_target="tpu_custom_call" | custom-call | tf_op jit(solution)/shard_map/pallas_call | solution.py:315
  178.8 15.0 %all_to_all.32 = f32[64,8,128]{2,1,0:T(8,128)S(1)} all-to-all(f32[64,8,128]{2,1,0:T(8,128)S(1)} %bitcast.48), channel_id=1, replica_groups=mesh['x'=4,'zh'=8,'zl'=2,'y'=4,'k'=2] {'x','zl','k','y'}, dimensions={0} | all-to-all | bytes 524288 | tf_op jit(solution)/shard_map/all_to_all | solution.py:289
  193.8 24.9 %all_gather.11 = f32[8,128,128]{2,1,0:T(8,128)S(1)} all-gather(f32[1,128,128]{2,1,0:T(8,128)S(1)} %bitcast.54), channel_id=1, replica_groups=mesh['x'=4,'zh'=8,'zl'=2,'y'=4,'k'=2] {'zh'}, dimensions={0}, use_global_device_ids=true | all-gather | bytes 589824 | tf_op jit(solution)/shard_map/all_gather | solution.py:305
  218.7 2.6 shard_map.64
  221.3 35.1 %all_to_all.33 = f32[64,56,128]{2,1,0:T(8,128)} all-to-all(f32[64,56,128]{2,1,0:T(8,128)S(1)} %bitcast.41), channel_id=1, replica_groups=mesh['x'=4,'zh'=8,'zl'=2,'y'=4,'k'=2] {'x','zl','k','y'}, dimensions={0} | all-to-all | bytes 3670016 | tf_op jit(solution)/shard_map/all_to_all | solution.py:289
  256.5 4.2 %shard_map.65 = (f32[4,3,128,128]{3,2,1,0:T(8,128)S(1)}, f32[4,3,128,128]{3,2,1,0:T(8,128)S(1)}, f32[128,128]{1,0:T(8,128)}) custom-call(s32[2]{0:T(128)S(1)} %pad_add_fusion.at, f32[3584,128]{1,0:T(8,128)} %bitcast.50, f32[4,6,128,128]{3,2,1,0:T(8,128)S(1)} %get-tuple-element.17.tiles, f32[128,128]{1,0:T(8,128)S(1)} %get-tuple-element.18.diag, ...), custom_call_target="tpu_custom_call" | custom-call | tf_op jit(solution)/shard_map/pallas_call | solution.py:317
  260.6 3.5 %collective-permute-start.1 = (f32[4,3,128,128]{3,2,1,0:T(8,128)S(1)}, f32[4,3,128,128]{3,2,1,0:T(8,128)S(1)}, u32[]{:S(2)}, u32[]{:S(2)}) collective-permute-start(f32[4,3,128,128]{3,2,1,0:T(8,128)S(1)} %get-tuple-element.20), channel_id=1, source_target_pairs={{0,1},{1,0},{2,3},{3,2},{4,5},{5,4},{6,7},{7,6},{8,9},{9,8},{10,11... | collective-permute-start | bytes 2359304 | tf_op jit(solution)/shard_map/ppermute | solution.py:284
  264.2 1.9 collective-permute-done.1
  266.0 0.1 select_bitcast_fusion.1
  266.2 0.1 pad_maximum_fusion
  266.3 1.3 copy.15
  (4 shorter events, 0.1 us)
Async XLA Ops:
  0.6 0.8 copy-start.2
  1.5 0.7 copy-start.3
  3.5 19.3 %all-to-all-start = ((f32[64,4,128]{2,1,0:T(4,128)}), f32[64,4,128]{2,1,0:T(4,128)S(1)}, u32[]{:S(2)}, u32[]{:S(2)}) async-start(f32[64,4,128]{2,1,0:T(4,128)} %bitcast.3), calls=%async_computation | async-start | bytes 262144 | tf_op jit(solution)/shard_map/all_to_all | solution.py:289
  57.9 10.4 %copy-start = (f32[8,3,128,128]{3,2,1,0:T(8,128)S(1)}, f32[8,3,128,128]{3,2,1,0:T(8,128)}, u32[]{:S(2)}) copy-start(f32[8,3,128,128]{3,2,1,0:T(8,128)} %tiles.1) | copy-start | bytes 4718596
  58.0 35.3 %all-to-all-start.1 = ((f32[64,56,128]{2,1,0:T(8,128)}), f32[64,56,128]{2,1,0:T(8,128)}, u32[]{:S(2)}, u32[]{:S(2)}) async-start(f32[64,56,128]{2,1,0:T(8,128)} %bitcast.7), calls=%async_computation.1 | async-start | bytes 3670016 | tf_op jit(solution)/shard_map/all_to_all | solution.py:289
  68.3 25.0 %copy-start.1 = (f32[128,128]{1,0:T(8,128)S(1)}, f32[128,128]{1,0:T(8,128)}, u32[]{:S(2)}) copy-start(f32[128,128]{1,0:T(8,128)} %diag.3) | copy-start | bytes 196612
  68.4 4.4 %collective-permute-start = (f32[4,3,128,128]{3,2,1,0:T(8,128)S(1)}, f32[4,3,128,128]{3,2,1,0:T(8,128)S(1)}, u32[]{:S(2)}, u32[]{:S(2)}) collective-permute-start(f32[4,3,128,128]{3,2,1,0:T(8,128)S(1)} %fusion.1), channel_id=1, source_target_pairs={{0,1},{1,0},{2,3},{3,2},{4,5},{5,4},{6,7},{7,6},{8,9},{9,8},{10,11... | collective-permute-start | bytes 2359304 | tf_op jit(solution)/shard_map/ppermute | solution.py:284
  260.6 5.4 %collective-permute-start.1 = (f32[4,3,128,128]{3,2,1,0:T(8,128)S(1)}, f32[4,3,128,128]{3,2,1,0:T(8,128)S(1)}, u32[]{:S(2)}, u32[]{:S(2)}) collective-permute-start(f32[4,3,128,128]{3,2,1,0:T(8,128)S(1)} %get-tuple-element.20), channel_id=1, source_target_pairs={{0,1},{1,0},{2,3},{3,2},{4,5},{5,4},{6,7},{7,6},{8,9},{9,8},{10,11... | collective-permute-start | bytes 2359304 | tf_op jit(solution)/shard_map/ppermute | solution.py:284
